TPU v7x, 768 devices: a whole 4x8x12 slice. The times are simulated.
768 devices in a mesh: dp: 12 (over z), hidden: 64 (over y, x, core).
Axes of the slice: x: 4, y: 8, z: 12, core: 2. Of those that a mesh axis runs over, the one named last changes fastest.
Arguments:
- tokens: bfloat16 [384, 4096], P('dp', 'hidden'), may hold values from -6 to 6
- grad_out: bfloat16 [384, 4096], P('dp', 'hidden'), may hold values from -6 to 6
- routes: int32 [384, 2], P('dp'), may hold values from 0 to 5, all different within a row; in each aligned block of 32 rows (0 to 31, 32 to 63, ...) at most 20 rows name the same one
- probs: bfloat16 [384, 2], P('dp'), may hold values from 0.099609375 to 0.8984375
- gate_weight: bfloat16 [86016, 4096], P(('dp', 'hidden')), may hold values from -0.09375 to 0.09375
- up_weight: bfloat16 [86016, 4096], P(('dp', 'hidden')), may hold values from -0.09375 to 0.09375
- down_weight: bfloat16 [86016, 4096], P(('dp', 'hidden')), may hold values from -0.0625 to 0.0625
Outputs:
- grad_tokens: bfloat16 [384, 4096], P('dp', 'hidden')
- grad_probs: float32 [384, 2], P('dp')
- grad_gate: bfloat16 [86016, 4096], P(('dp', 'hidden'))
- grad_up: bfloat16 [86016, 4096], P(('dp', 'hidden'))
Inputs may be any that keep to these rules, and one draw needn't show every extreme that they name: `routes`: A token's two experts differ. Among the 32 tokens of one index of dp no expert is named more than 20 times, a bound that some block reaches.
All inputs are finite; a program needn't handle non-finite values.
Results may differ from a plain program's by a relative error of at most 0.0049.
Values may be sent and summed in bfloat16 or wider, within the bound.
No kernel may reach another device: no remote copies, remote signals or barrier semaphores. Data moves between devices by JAX's collectives and lax.ppermute only.
A program may use at most 128 MiB of HBM per device.

v0:
```python
import jax
import jax.numpy as jnp
from jax import lax
from jax.sharding import PartitionSpec as P

CAP = 20


def body(tokens, grad_out, routes, probs, gate_weight, up_weight, down_weight):
    dp_count = lax.axis_size("dp")
    hidden_count = lax.axis_size("hidden")
    large_count = dp_count // 6
    expert_total = dp_count - 3 * large_count
    block_ids = jnp.arange(dp_count, dtype=jnp.int32)
    owners = jnp.where(block_ids < 4 * large_count, block_ids // 4, block_ids - 3 * large_count)
    expert_hits = (
        routes[:, :, None] == jnp.arange(expert_total, dtype=jnp.int32)[None, None, :]
    ).astype(jnp.int32)
    per_token = jnp.sum(expert_hits, axis=1)
    before = jnp.cumsum(per_token, axis=0) - per_token
    slot_rank = jnp.sum(expert_hits * before[:, None, :], axis=2)
    matches = routes[:, :, None] == owners[None, None, :]
    slot_hits = slot_rank[:, :, None, None] == jnp.arange(CAP, dtype=jnp.int32)[None, None, None, :]
    picked = (matches[:, :, :, None] & slot_hits).astype(jnp.float32)
    select = jnp.sum(picked, axis=1)
    select_half = select.astype(jnp.bfloat16)
    send_tokens = jnp.einsum(
        "tjc,td->jcd", select_half, tokens, preferred_element_type=jnp.float32
    ).astype(jnp.bfloat16)
    send_grads = jnp.einsum(
        "tjc,td->jcd", select_half, grad_out, preferred_element_type=jnp.float32
    ).astype(jnp.bfloat16)
    send_probs = jnp.einsum(
        "tkjc,tk->jc", picked, probs.astype(jnp.float32), precision=lax.Precision.HIGHEST
    ).astype(jnp.bfloat16)
    recv_tokens, recv_grads, recv_probs = (
        lax.all_to_all(send_tokens, "dp", split_axis=0, concat_axis=0, tiled=True),
        lax.all_to_all(send_grads, "dp", split_axis=0, concat_axis=0, tiled=True),
        lax.all_to_all(send_probs, "dp", split_axis=0, concat_axis=0, tiled=True),
    )
    row_count = dp_count * CAP
    contract = (((1,), (1,)), ((), ()))
    full_tokens, full_grads = (
        lax.all_gather(recv_tokens, "hidden", axis=2, tiled=True),
        lax.all_gather(recv_grads, "hidden", axis=2, tiled=True),
    )
    token_rows = full_tokens.reshape(row_count, full_tokens.shape[2])
    grad_rows = full_grads.reshape(row_count, full_grads.shape[2])
    back_pre = lax.dot_general(grad_rows, down_weight, contract, preferred_element_type=jnp.float32)
    slot_probs = recv_probs.reshape(row_count).astype(jnp.float32)
    gate_pre = lax.dot_general(
        token_rows, gate_weight, contract, preferred_element_type=jnp.float32
    )
    up_pre = lax.dot_general(token_rows, up_weight, contract, preferred_element_type=jnp.float32)
    sigmoid_gate = jax.nn.sigmoid(gate_pre)
    silu_gate = gate_pre * sigmoid_gate
    router_part = jnp.sum(silu_gate * up_pre * back_pre, axis=1)
    scaled = slot_probs[:, None] * back_pre
    grad_gate_pre = (
        scaled * up_pre * sigmoid_gate * (1.0 + gate_pre * (1.0 - sigmoid_gate))
    ).astype(jnp.bfloat16)
    grad_up_pre = (scaled * silu_gate).astype(jnp.bfloat16)
    over_rows = (((0,), (0,)), ((), ()))
    grad_gate = lax.dot_general(
        grad_gate_pre, token_rows, over_rows, preferred_element_type=jnp.float32
    ).astype(jnp.bfloat16)
    grad_up = lax.dot_general(
        grad_up_pre, token_rows, over_rows, preferred_element_type=jnp.float32
    ).astype(jnp.bfloat16)
    feature_width = gate_weight.shape[1] // hidden_count
    cross = (((0,), (1,)), ((), ()))
    own_features = lax.psum_scatter(
        lax.dot_general(gate_weight, grad_gate_pre, cross, preferred_element_type=jnp.float32)
        + lax.dot_general(up_weight, grad_up_pre, cross, preferred_element_type=jnp.float32),
        "hidden",
        scatter_dimension=0,
        tiled=True,
    ).T
    router_payload = lax.psum(router_part, "hidden")
    back_features, back_router = (
        lax.all_to_all(
            own_features.reshape(dp_count, CAP, feature_width),
            "dp",
            split_axis=0,
            concat_axis=0,
            tiled=True,
        ),
        lax.all_to_all(
            router_payload.reshape(dp_count, CAP), "dp", split_axis=0, concat_axis=0, tiled=True
        ),
    )
    token_router = jnp.einsum("tkjc,jc->tk", picked, back_router, precision=lax.Precision.HIGHEST)
    grad_tokens = jnp.einsum(
        "tjc,jcd->td", select, back_features, precision=lax.Precision.HIGHEST
    ).astype(jnp.bfloat16)
    return (grad_tokens, token_router, grad_gate, grad_up)


def solution(mesh):
    placed = (
        P("dp", "hidden"),
        P("dp", "hidden"),
        P("dp", None),
        P("dp", None),
        P(("dp", "hidden"), None),
        P(("dp", "hidden"), None),
        P(("dp", "hidden"), None),
    )
    return jax.shard_map(
        body,
        mesh=mesh,
        in_specs=placed,
        out_specs=(
            P("dp", "hidden"),
            P("dp", None),
            P(("dp", "hidden"), None),
            P(("dp", "hidden"), None),
        ),
        check_vma=False,
    )
```

profile of v0, /device:TPU:1, one launch (start us, length us, event | category | flops | bytes accessed | tf_op | source)
XLA Modules:
  0.0 469.9 jit_solution(4094957973058879481)
XLA Ops:
  7.2 0.0 copy-start
  7.2 0.0 copy-start.4
  7.2 0.0 all-gather.5.cloned.1.call-start
  7.2 0.8 convert_reduce_fusion.2
  8.0 0.8 broadcast_compare_fusion
  8.8 0.1 copy.26
  8.9 0.1 reduce_window_sum.11
  8.9 0.1 copy.28
  9.0 0.7 select_reduce_fusion
  9.7 0.4 convert_reduce_fusion
  10.1 0.9 convolution_convert_fusion.2
  11.0 0.1 reshape.86
  11.1 24.9 %all_to_all.36 = bf16[12,2,640]{2,1,0:T(2,128)(2,1)S(1)} all-to-all(bf16[12,2,640]{2,1,0:T(2,128)(2,1)S(1)} %reshape.86), channel_id=1, replica_groups=mesh['dp'=12,'hidden'=64] {'dp'}, dimensions={0} | all-to-all | bytes 61440 | tf_op jit(solution)/shard_map/all_to_all | solution.py:37
  36.0 0.1 reshape.87
  36.1 1.0 copy.32
  37.1 0.0 all-gather.5.cloned.1.call-update
  37.1 0.0 all-gather.3.cloned.1.call-start
  37.2 0.9 convolution_convert_fusion.3
  38.0 0.1 reshape.88
  38.1 11.9 %all_to_all.37 = bf16[12,2,640]{2,1,0:T(2,128)(2,1)S(1)} all-to-all(bf16[12,2,640]{2,1,0:T(2,128)(2,1)S(1)} %reshape.88), channel_id=1, replica_groups=mesh['dp'=12,'hidden'=64] {'dp'}, dimensions={0} | all-to-all | bytes 61440 | tf_op jit(solution)/shard_map/all_to_all | solution.py:38
  50.0 0.1 reshape.89
  50.1 1.0 copy.30
  51.1 0.0 all-gather.3.cloned.1.call-update
  51.1 0.0 reduce-scatter.4.cloned.1.call-start
  51.2 0.1 broadcast_and_fusion
  51.3 0.0 copy-start.2
  51.3 0.6 copy-done.2
  51.9 0.0 copy-done.4
  52.0 0.2 fusion.2
  52.2 11.4 %all_to_all.38 = bf16[12,1,20]{2,1,0:T(2,128)(2,1)S(1)} all-to-all(bf16[12,1,20]{2,1,0:T(2,128)(2,1)S(1)} %copy.29), channel_id=1, replica_groups=mesh['dp'=12,'hidden'=64] {'dp'}, dimensions={0} | all-to-all | bytes 960 | tf_op jit(solution)/shard_map/all_to_all | solution.py:39
  63.6 0.1 reshape.72
  63.7 79.7 %all-gather.5.cloned.1.call-done = bf16[12,20,4096]{1,0,2:T(8,128)(2,1)} async-done(((bf16[12,20,64]{1,0,2:T(8,128)(2,1)}), bf16[12,20,4096]{1,0,2:T(8,128)(2,1)}) %all-gather.5.cloned.1.call-update) | async-done | bytes 1966096 | tf_op jit(solution)/shard_map/all_gather | solution.py:44
  143.4 18.8 %reshape.81 = bf16[240,4096]{0,1:T(8,128)(2,1)S(1)} reshape(bf16[12,20,4096]{1,0,2:T(8,128)(2,1)} %all-gather.5.cloned.1.call-done) | data formatting | bytes 3932160 | tf_op jit(solution)/shard_map/reshape | solution.py:47
  162.3 1.7 fusion.14
  163.9 0.0 copy-done
  163.9 0.4 fusion.15
  164.4 91.4 %all-gather.3.cloned.1.call-done = bf16[12,20,4096]{1,0,2:T(8,128)(2,1)} async-done(((bf16[12,20,64]{1,0,2:T(8,128)(2,1)}), bf16[12,20,4096]{1,0,2:T(8,128)(2,1)}) %all-gather.3.cloned.1.call-update) | async-done | bytes 1966096 | tf_op jit(solution)/shard_map/all_gather | solution.py:45
  255.8 20.0 %reshape.80 = bf16[240,4096]{0,1:T(8,128)(2,1)} reshape(bf16[12,20,4096]{1,0,2:T(8,128)(2,1)} %all-gather.3.cloned.1.call-done) | data formatting | bytes 3932160 | tf_op jit(solution)/shard_map/reshape | solution.py:48
  275.8 2.4 multiply_reduce_fusion
  278.1 0.0 copy-start.1
  278.2 0.7 fusion.13
  278.8 0.5 copy-done.1
  279.3 2.6 fusion
  281.9 5.5 %copy.42 = f32[4096,240]{1,0:T(8,128)} copy(f32[4096,240]{0,1:T(8,128)} %fusion) | data formatting | bytes 7864320
  287.4 0.0 reduce-scatter.4.cloned.1.call-update
  287.4 0.1 all_to_all.28
  287.5 126.4 %psum.7 = f32[12,1,20]{2,1,0:T(1,128)} all-reduce(f32[12,1,20]{2,1,0:T(1,128)S(1)} %all_to_all.28), channel_id=1, replica_groups=mesh['dp'=12,'hidden'=64] {'hidden'}, use_global_device_ids=true, to_apply=%region_6.7 | all-reduce | flops 240 | bytes 1920 | tf_op jit(solution)/shard_map/psum | solution.py:79
  413.9 9.9 %all-to-all-start.4 = ((f32[12,1,20]{2,1,0:T(1,128)}), f32[12,1,20]{2,1,0:T(1,128)S(1)}, u32[]{:S(2)}, u32[]{:S(2)}) async-start(f32[12,1,20]{2,1,0:T(1,128)} %psum.7), calls=%async_computation.4 | async-start | bytes 12288 | tf_op jit(solution)/shard_map/all_to_all | solution.py:88
  423.8 1.7 convolution_convert_fusion.1
  425.5 0.0 copy-start.3
  425.5 1.7 convolution_convert_fusion
  427.2 12.9 %reduce-scatter.4.cloned.1.call-done = f32[64,240]{1,0:T(8,128)} async-done(((f32[4096,240]{1,0:T(8,128)}), f32[64,240]{1,0:T(8,128)}) %reduce-scatter.4.cloned.1.call-update) | async-done | bytes 61456
  440.1 0.9 copy.43
  441.1 0.7 reshape.90
  441.8 0.0 all-to-all-done.4
  441.8 9.6 %all-to-all-start.3 = ((f32[12,1,1280]{2,1,0:T(1,128)}), f32[12,1,1280]{2,1,0:T(1,128)S(1)}, u32[]{:S(2)}, u32[]{:S(2)}) async-start(f32[12,1,1280]{2,1,0:T(1,128)} %reshape.90), calls=%async_computation.3 | async-start | bytes 122880 | tf_op jit(solution)/shard_map/all_to_all | solution.py:81
  451.4 0.0 copy-done.3
  451.4 0.8 fusion.4
  452.2 8.7 %all-to-all-done.3 = f32[12,1,1280]{2,1,0:T(1,128)S(1)} async-done(((f32[12,1,1280]{2,1,0:T(1,128)}), f32[12,1,1280]{2,1,0:T(1,128)S(1)}, u32[]{:S(2)}, u32[]{:S(2)}) %all-to-all-start.3) | async-done | bytes 61472 | tf_op jit(solution)/shard_map/all_to_all | solution.py:81
  461.0 0.5 broadcast.87
  461.5 0.8 reduce.2
  462.3 0.1 reshape.91
  462.4 1.0 fusion.1
  (7 shorter events, 0.1 us)
Async XLA Ops:
  7.2 156.8 %copy-start = (bf16[112,4096]{1,0:T(8,128)(2,1)S(1)}, bf16[112,4096]{1,0:T(8,128)(2,1)}, u32[]{:S(2)}) copy-start(bf16[112,4096]{1,0:T(8,128)(2,1)} %param.11) | copy-start | bytes 2752516
  7.2 44.8 %copy-start.4 = (bf16[32,2]{0,1:T(2,128)(2,1)S(1)}, bf16[32,2]{0,1:T(2,128)(2,1)}, u32[]{:S(2)}) copy-start(bf16[32,2]{0,1:T(2,128)(2,1)} %param.10) | copy-start | bytes 388
  7.2 136.2 %all-gather.5.cloned.1.call-start = ((), (), s32[]{:S(2)}) async-start(), calls=%async_computation.7 | async-start | bytes 17039360 | tf_op jit(solution)/shard_map/all_gather | solution.py:44
  37.1 218.7 %all-gather.3.cloned.1.call-start = ((), (), s32[]{:S(2)}) async-start(), calls=%async_computation.6 | async-start | bytes 17039360 | tf_op jit(solution)/shard_map/all_gather | solution.py:45
  51.1 389.0 %reduce-scatter.4.cloned.1.call-start = ((), (), s32[]{:S(2)}) async-start(), calls=%async_computation.8 | async-start | bytes 4259840
  51.3 0.6 copy-start.2
  278.1 1.2 copy-start.1
  413.9 28.0 %all-to-all-start.4 = ((f32[12,1,20]{2,1,0:T(1,128)}), f32[12,1,20]{2,1,0:T(1,128)S(1)}, u32[]{:S(2)}, u32[]{:S(2)}) async-start(f32[12,1,20]{2,1,0:T(1,128)} %psum.7), calls=%async_computation.4 | async-start | bytes 12288 | tf_op jit(solution)/shard_map/all_to_all | solution.py:88
  425.5 25.9 %copy-start.3 = (pred[32,2,12,20]{0,1,3,2:T(4,128)(4,1)S(1)}, pred[32,2,12,20]{0,1,3,2:T(4,128)(4,1)}, u32[]{:S(2)}) copy-start(pred[32,2,12,20]{0,1,3,2:T(4,128)(4,1)} %copy-done.2) | copy-start | bytes 46084
  441.8 19.1 %all-to-all-start.3 = ((f32[12,1,1280]{2,1,0:T(1,128)}), f32[12,1,1280]{2,1,0:T(1,128)S(1)}, u32[]{:S(2)}, u32[]{:S(2)}) async-start(f32[12,1,1280]{2,1,0:T(1,128)} %reshape.90), calls=%async_computation.3 | async-start | bytes 122880 | tf_op jit(solution)/shard_map/all_to_all | solution.py:81
Sparse Core Ops, SparseCore 0:
  37.2 106.1 all-gather.4
  147.9 107.8 all-gather.2
  287.5 152.5 reduce-scatter.3
where the time goes:
time: 477 us; the launch traced here: 470 us
  waiting for transfers between devices  193 us (40%)
  blocking collectives  175 us (37%)
  local copies, waits for them, and re-layouts  50.4 us (11%)
  starting transfers between devices  19.6 us (4%)
  matrix products  14.9 us (3%)
  between operations  13.9 us (3%)
    psum x1, blocking collectives, body(): router_payload = lax.psum(router_part, 'hidden')  126 us
    all_gather x1, waiting for transfers between devices, body(): lax.all_gather(recv_grads, 'hidden', axis=2, tiled=True)  91.4 us
    all_gather x1, waiting for transfers between devices, body(): lax.all_gather(recv_tokens, 'hidden', axis=2, tiled=True)  79.7 us
    all_to_all x1, blocking collectives, body(): lax.all_to_all(send_tokens, 'dp', split_axis=0, concat_axis=0, tiled=True)  24.9 us
    reshape x1, local copies, waits for them, and re-layouts, body(): grad_rows = full_grads.reshape(row_count, full_grads.shape[2])  20 us
    reshape x1, local copies, waits for them, and re-layouts, body(): token_rows = full_tokens.reshape(row_count, full_tokens.shape[2])  18.8 us
    unnamed x4, waiting for transfers between devices  13 us
    all_to_all x1, blocking collectives, body(): lax.all_to_all(send_grads, 'dp', split_axis=0, concat_axis=0, tiled=True)  11.9 us
  transfers between devices with their start and end apart: 5, of which 4 were waited for; matrix products, arithmetic and copies ran while one was open for 6% of the time, Pallas kernels for 0%

commit v1 on v0

v1 whole, which is shorter than its diff:
```python
import jax
import jax.numpy as jnp
from jax import lax
from jax.experimental import pallas as pl
from jax.experimental.pallas import tpu as pltpu
from jax.sharding import Mesh, PartitionSpec as P

DP = 12
CAP = 20
SLOTS = 256
ROWS = 24
BACK = 16
BF = jnp.bfloat16
F32 = jnp.float32
VMEM = pl.BlockSpec(memory_space=pltpu.VMEM)
PLANE = ("yl", "x")
FAR = ("dp", "yh")


def iota(shape, dim):
    return lax.broadcasted_iota(jnp.int32, shape, dim)


def by24(r):
    return (r * 171) >> 12


def by20(s):
    return (s * 205) >> 12


def owner_of(j):
    return jnp.where(j < 8, j >> 2, j - 6)


def dot(a, b, ca, cb, precision=None):
    return lax.dot_general(
        a, b, (((ca,), (cb,)), ((), ())), preferred_element_type=F32, precision=precision
    )


def one_hot(mask):
    return jnp.where(mask, 1.0, 0.0)


def select_kernel(routes, probs, tokens_hbm, grads_hbm, out, tokens, grads, sems):
    copies = [
        pltpu.make_async_copy(tokens_hbm, tokens, sems.at[0]),
        pltpu.make_async_copy(grads_hbm, grads, sems.at[1]),
    ]
    for a in copies:
        a.start()
    rows = DP * ROWS
    r = iota((rows, 32), 0)
    j = by24(r)
    c = r - ROWS * j
    owner = owner_of(j)
    first = routes[0:1, :] == owner
    second = routes[1:2, :] == owner
    hit = one_hot(first | second)
    earlier = one_hot(iota((32, 32), 0) < iota((32, 32), 1)).astype(BF)
    rank = dot(hit.astype(BF), earlier, 1, 0)
    chosen = hit * one_hot(rank == c.astype(F32))
    p = probs[...].astype(F32)
    weight = jnp.sum(chosen * jnp.where(first, p[0:1, :], p[1:2, :]), axis=1, keepdims=True)
    for a in copies:
        a.wait()
    values = jnp.concatenate([tokens[...].astype(F32), grads[...].astype(F32)], axis=1)
    picked = dot(chosen.astype(BF), values.astype(BF), 1, 0)
    rl = iota((rows, 128), 0)
    at_lane = one_hot(rl - ROWS * by24(rl) == iota((rows, 128), 1))
    ra, rb = iota((rows, rows), 0), iota((rows, rows), 1)
    ja = by24(ra)
    gather = one_hot((ra - ROWS * ja == CAP) & (ja == by24(rb)))
    picked += dot(gather.astype(BF), (weight * at_lane).astype(BF), 1, 0)
    block = picked.reshape(DP, ROWS, 128).astype(BF)
    for k in range(4):
        out[:, k] = block


def spread_kernel(recv, out, prob, held):
    rows = DP * ROWS

    @pl.when(pl.program_id(0) == 0)
    def _():
        r, s = iota((rows, SLOTS), 0), iota((rows, SLOTS), 1)
        i = by20(s)
        used = s < DP * CAP
        place = one_hot((r == ROWS * i + (s - CAP * i)) & used).astype(BF)
        for k in range(4):
            block = recv[:, k].astype(F32).reshape(rows, 128).astype(BF)
            held[k] = dot(block, place, 0, 0).astype(BF)
        block = recv[:, 0].astype(F32).reshape(rows, 128).astype(BF)
        lane, sl = iota((128, SLOTS), 0), iota((128, SLOTS), 1)
        fan = one_hot(lane == sl - CAP * by20(sl)).astype(BF)
        fanned = dot(block, fan, 1, 0)
        prob[...] = jnp.sum(
            jnp.where((r == ROWS * i + CAP) & used, fanned, 0.0), axis=0, keepdims=True
        )

    out[0] = held[...]


def place_copies(core, mine, other, held, sems):
    copies = []
    for k in range(8):
        for n, src in enumerate((mine, other)):
            slot = core if n == 0 else 1 - core
            copies.append(
                pltpu.make_async_copy(
                    src.at[k, :, pl.ds(0, 64), :], held.at[:, k, slot], sems.at[2 * k + n]
                )
            )
    return copies


def split(v):
    high = v.astype(BF).astype(F32)
    return high, v - high


def two_rows(v):
    high, low = split(v)
    n = iota((16, SLOTS), 0)
    return jnp.where(n == 0, high, jnp.where(n == 1, low, 0.0)).astype(BF)


def hidden_part(w, x, k):
    at = pl.ds(256 * k, 256)
    tokens = x[k, :, 0:64, :].reshape(256, SLOTS)
    grads = x[k, :, 64:128, :].reshape(256, SLOTS)
    return dot(w[0:224, at], tokens, 1, 0), dot(w[224:336, at], grads, 1, 0)


def own_kernel(core_ref, mine, wg, wu, wd, w_own, w_other, part, w, sems):
    core = core_ref[0]
    copies = []
    for n, src in enumerate((wg, wu, wd)):
        for q in range(4):
            at = pl.ds(1024 * q, 1024)
            dst = w.at[pl.ds(112 * n, 112), at]
            copies.append(pltpu.make_async_copy(src.at[:, at], dst, sems.at[4 * n + q]))
    for a in copies:
        a.start()
    for a in copies:
        a.wait()
    both = jnp.zeros((224, SLOTS), F32)
    back = jnp.zeros((112, SLOTS), F32)
    for k in range(8):
        blocks = [w[:, (yh * 8 + k) * 128 : (yh * 8 + k + 1) * 128] for yh in range(4)]
        low = jnp.concatenate([v[:, 0:64] for v in blocks], axis=1)
        high = jnp.concatenate([v[:, 64:128] for v in blocks], axis=1)
        at = pl.ds(256 * k, 256)
        w_own[:, at] = jnp.where(core == 0, low, high)
        w_other[:, at] = jnp.where(core == 0, high, low)
        b, r = hidden_part(w_own, mine, k)
        both += b
        back += r
    part[0:224] = both
    part[224:336] = back


def main_kernel(other, part, prob, w_other, send, pre, terms):
    both, back = part[0:224], part[224:336]
    for k in range(8):
        b, r = hidden_part(w_other, other, k)
        both += b
        back += r
    gate, up = both[0:112], both[112:224]
    sig = jax.nn.sigmoid(gate)
    silu = gate * sig
    router = two_rows(jnp.sum(silu * up * back, axis=0, keepdims=True))
    scaled = prob[...] * back
    d_gate = (scaled * up * sig * (1.0 + gate * (1.0 - sig))).astype(BF)
    d_up = (scaled * silu).astype(BF)
    grads = jnp.concatenate([d_gate, d_up], axis=0)
    pre[...] = grads
    terms[...] = router
    for k in range(8):
        send[k, 0:256] = dot(w_other[0:224, pl.ds(256 * k, 256)], grads, 0, 0).astype(BF)
        send[k, 256:272] = router


def keep_kernel(w_own, pre, keep):
    for k in range(8):
        keep[k] = dot(w_own[0:224, pl.ds(256 * k, 256)], pre[...], 0, 0)


def weight_kernel(core_ref, mine, other, pre, out_gate, out_up, xt, xsem):
    core = core_ref[0]
    copies = place_copies(core, mine, other, xt, xsem)
    for a in copies:
        a.start()
    for k in range(8):
        copies[2 * k].wait()
        copies[2 * k + 1].wait()
        part = dot(pre[...], xt[:, k].reshape(512, SLOTS), 1, 1).astype(BF)
        for yh in range(4):
            at = pl.ds((yh * 8 + k) * 128, 128)
            out_gate[:, at] = part[0:112, yh * 128 : (yh + 1) * 128]
            out_up[:, at] = part[112:224, yh * 128 : (yh + 1) * 128]


def add_kernel(keep, own_terms, swapped, out):
    out[0, 0:256] = (keep[0] + swapped[0, 0:256].astype(F32)).astype(BF)
    terms = own_terms[...].astype(F32) + swapped[0, 256:272].astype(F32)
    out[0, 256:272] = two_rows(jnp.sum(terms, axis=0, keepdims=True))


def return_kernel(recv, out):
    rows = DP * BACK
    total = recv[0, 0:256].astype(F32)
    terms = recv[0, 256:272].astype(F32)
    for k in range(1, 8):
        total += recv[k, 0:256].astype(F32)
        terms += recv[k, 256:272].astype(F32)
    high, low = split(jnp.sum(terms, axis=0, keepdims=True))
    r, s = iota((rows, SLOTS), 0), iota((rows, SLOTS), 1)
    i, c = r >> 4, r & 15
    in_block = (by20(s) == i) & (s < DP * CAP)
    slot = s - CAP * i
    left = one_hot(in_block & (slot == c) & (c < 10)).astype(BF)
    right = one_hot(in_block & (slot == c + 10) & (c < 10)).astype(BF)
    spread = jnp.where(in_block & (c == 10), high, jnp.where(in_block & (c == 11), low, 0.0))
    sl, lane = iota((SLOTS, 128), 0), iota((SLOTS, 128), 1)
    fan = one_hot(sl - CAP * by20(sl) == lane).astype(BF)
    terms_part = dot(spread.astype(BF), fan, 1, 0)
    empty = jnp.zeros((64, SLOTS), BF)
    for yh in range(4):
        block = total[yh * 64 : (yh + 1) * 64].astype(BF)
        part = terms_part + dot(left, jnp.concatenate([block, empty], axis=0), 1, 1)
        part += dot(right, jnp.concatenate([empty, block], axis=0), 1, 1)
        out[:, yh] = part.reshape(DP, BACK, 128).astype(BF)


def combine_kernel(routes, recv, grad_tokens, grad_probs):
    cols = DP * 4 * BACK
    eye = one_hot(iota((32, 32), 0) == iota((32, 32), 1))
    place = dot(eye.astype(BF), routes[...].astype(F32).astype(BF), 1, 1)
    first, second = place[:, 0:1], place[:, 1:2]
    r = iota((32, cols), 1)
    c = (r & 15).astype(F32)
    owner = owner_of(r >> 6).astype(F32)
    hit = one_hot((first == owner) | (second == owner))
    before = one_hot(iota((32, 32), 1) < iota((32, 32), 0)).astype(BF)
    rank = dot(before, hit.astype(BF), 1, 0)
    paired = hit * one_hot(c < 10.0)
    chosen = jnp.concatenate(
        [paired * one_hot(rank == c), paired * one_hot(rank == c + 10.0)], axis=0
    )
    rows = recv[...].reshape(cols, 128)
    both = dot(chosen.astype(BF), rows, 1, 0)
    grad_tokens[...] = (both[0:32, 0:64] + both[32:64, 64:128]).astype(BF)
    lane = iota((32, 128), 1).astype(F32)
    sums = [jnp.zeros((32, 128), F32), jnp.zeros((32, 128), F32)]
    for j in range(DP):
        terms = jnp.sum(recv[j].astype(F32), axis=0)
        term = terms[10:11] + terms[11:12]
        owner_j = float(j // 4 if j < 8 else j - 6)
        here = jnp.where(rank[:, 64 * j : 64 * j + 1] == lane, term, 0.0)
        sums[0] += jnp.where(first == owner_j, here, 0.0)
        sums[1] += jnp.where(second == owner_j, here, 0.0)
    ones = jnp.ones((8, 128), F32)
    for n in range(2):
        row = dot(ones, sums[n], 1, 1, lax.Precision.HIGHEST)
        grad_probs[n : n + 1, :] = row[0:1, :]


def params():
    return pltpu.CompilerParams(vmem_limit_bytes=40 * 1024 * 1024)


def shape(dims, dtype):
    return jax.ShapeDtypeStruct(dims, dtype)


def body(tokens, grad_out, routes, probs, gate_weight, up_weight, down_weight):
    any_space = pl.BlockSpec(memory_space=pl.ANY)
    smem = pl.BlockSpec(memory_space=pltpu.SMEM)
    core = lax.axis_index("core").astype(jnp.int32).reshape(1)
    routes_t = routes.T
    picked = pl.pallas_call(
        select_kernel,
        out_shape=shape((DP, 4, ROWS, 128), BF),
        in_specs=[VMEM, VMEM, any_space, any_space],
        out_specs=VMEM,
        scratch_shapes=[
            pltpu.VMEM((32, 64), BF),
            pltpu.VMEM((32, 64), BF),
            pltpu.SemaphoreType.DMA((2,)),
        ],
        compiler_params=params(),
        name="select_rows",
    )(routes_t, probs.T, tokens, grad_out)
    got = lax.all_to_all(picked.reshape(DP * 4, ROWS, 128), FAR, 0, 0, tiled=True)
    spread, prob = pl.pallas_call(
        spread_kernel,
        grid=(8,),
        out_shape=(shape((8, 4, 128, SLOTS), BF), shape((1, SLOTS), F32)),
        in_specs=[pl.BlockSpec((DP, 4, ROWS, 128), lambda n: (0, 0, 0, 0))],
        out_specs=(
            pl.BlockSpec((1, 4, 128, SLOTS), lambda n: (n, 0, 0, 0)),
            pl.BlockSpec((1, SLOTS), lambda n: (0, 0)),
        ),
        scratch_shapes=[pltpu.VMEM((4, 128, SLOTS), BF)],
        compiler_params=params(),
        name="spread_rows",
    )(got.reshape(DP, 4, ROWS, 128))
    mine = lax.all_to_all(spread, PLANE, 0, 0, tiled=True)
    swap = [(0, 1), (1, 0)]
    other = lax.ppermute(mine, "core", swap)
    held = pltpu.VMEM((4, 8, 2, 64, SLOTS), BF)
    w_own, w_other, part = pl.pallas_call(
        own_kernel,
        out_shape=(
            shape((336, 2048), BF),
            shape((336, 2048), BF),
            shape((336, SLOTS), F32),
        ),
        in_specs=[smem, VMEM] + [any_space] * 3,
        out_specs=(VMEM,) * 3,
        scratch_shapes=[pltpu.VMEM((336, 4096), BF), pltpu.SemaphoreType.DMA((12,))],
        compiler_params=params(),
        cost_estimate=pl.CostEstimate(
            flops=360_000_000, bytes_accessed=8_000_000, transcendentals=0
        ),
        name="own_features",
    )(core, mine, gate_weight, up_weight, down_weight)
    send, pre, terms = pl.pallas_call(
        main_kernel,
        out_shape=(shape((8, 272, SLOTS), BF), shape((224, SLOTS), BF), shape((16, SLOTS), BF)),
        in_specs=[VMEM] * 4,
        out_specs=(VMEM,) * 3,
        compiler_params=params(),
        cost_estimate=pl.CostEstimate(
            flops=600_000_000, bytes_accessed=5_000_000, transcendentals=30_000
        ),
        name="hidden_and_input_grads",
    )(other, part, prob, w_other)
    swapped = lax.ppermute(send, "core", swap)
    keep = pl.pallas_call(
        keep_kernel,
        out_shape=shape((8, 256, SLOTS), F32),
        in_specs=[VMEM] * 2,
        out_specs=VMEM,
        compiler_params=params(),
        cost_estimate=pl.CostEstimate(
            flops=240_000_000, bytes_accessed=3_000_000, transcendentals=0
        ),
        name="input_grads_kept",
    )(w_own, pre)
    grad_gate, grad_up = pl.pallas_call(
        weight_kernel,
        out_shape=(shape((112, 4096), BF),) * 2,
        in_specs=[smem, any_space, any_space, VMEM],
        out_specs=(VMEM,) * 2,
        scratch_shapes=[held, pltpu.SemaphoreType.DMA((16,))],
        compiler_params=params(),
        cost_estimate=pl.CostEstimate(
            flops=480_000_000, bytes_accessed=4_000_000, transcendentals=0
        ),
        name="weight_grads",
    )(core, mine, other, pre)
    piece = pl.BlockSpec((1, 272, SLOTS), lambda n: (n, 0, 0))
    summed = pl.pallas_call(
        add_kernel,
        grid=(8,),
        out_shape=shape((8, 272, SLOTS), BF),
        in_specs=[
            pl.BlockSpec((1, 256, SLOTS), lambda n: (n, 0, 0)),
            pl.BlockSpec((16, SLOTS), lambda n: (0, 0)),
            piece,
        ],
        out_specs=piece,
        compiler_params=params(),
        name="add_cores",
    )(keep, terms, swapped)
    parts = lax.all_to_all(summed, PLANE, 0, 0, tiled=True)
    back = pl.pallas_call(
        return_kernel,
        out_shape=shape((DP, 4, BACK, 128), BF),
        in_specs=[VMEM],
        out_specs=VMEM,
        compiler_params=params(),
        name="return_rows",
    )(parts)
    home = lax.all_to_all(back.reshape(DP * 4, BACK, 128), FAR, 0, 0, tiled=True)
    grad_tokens, grad_probs = pl.pallas_call(
        combine_kernel,
        out_shape=(shape((32, 64), BF), shape((2, 32), F32)),
        in_specs=[VMEM] * 2,
        out_specs=(VMEM,) * 2,
        compiler_params=params(),
        name="combine",
    )(routes_t, home.reshape(DP, 4, BACK, 128))
    return grad_tokens, grad_probs.T, grad_gate, grad_up


def solution(mesh):
    fine = Mesh(mesh.devices.reshape(DP, 4, 2, 4, 2), ("dp", "yh", "yl", "x", "core"))
    hidden = ("yh", "yl", "x", "core")
    rows = P(("dp",) + hidden, None)
    placed = (P("dp", hidden), P("dp", hidden), P("dp", None), P("dp", None), rows, rows, rows)
    return jax.shard_map(
        body,
        mesh=fine,
        in_specs=placed,
        out_specs=(P("dp", hidden), P("dp", None), rows, rows),
        check_vma=False,
    )
```

time: 477 us -> 135 us (0.28); the launches traced: 470 us -> 133 us
  waiting for transfers between devices: 193 us -> 13.1 us
  blocking collectives: 175 us -> 86.6 us
  local copies, waits for them, and re-layouts: 50.4 us -> 5.08 us
  matrix products: 14.9 us -> 0 us
  Pallas kernels: 0 us -> 13.4 us
  between operations: 13.9 us -> 0.77 us
  starting transfers between devices: 19.6 us -> 14.5 us
    all_gather x2 -> x0, waiting for transfers between devices: 171 us -> none  [the longest x1 91.4 us: body(): lax.all_gather(recv_grads, 'hidden', axis=2, tiled=True)]
    psum x1 -> x0, blocking collectives: 126 us -> none  [body(): router_payload = lax.psum(router_part, 'hidden')]
    reshape x3 -> x0, local copies, waits for them, and re-layouts: 38.8 us -> none  [the longest x1 20 us: body(): grad_rows = full_grads.reshape(row_count, full_grads.shape[2])]
    all_to_all x3, blocking collectives: 48.2 us -> 86.6 us  [the longest x1 40.9 us: body(): lax.all_to_all(picked.reshape(DP * 4, ROWS, 128), FAR, 0, 0, tiled=True)]
    dot_general x12 -> x0, matrix products: 14.9 us -> none  [the longest x1 2.56 us: body(): lax.dot_general(up_weight, grad_up_pre, cross, preferred_element_type=jnp...]
    all_to_all x2 -> x1, starting transfers between devices: 19.5 us -> 6 us  [body(): lax.all_to_all(back.reshape(DP * 4, BACK, 128), FAR, 0, 0, tiled=True)]
    pallas_call x0 -> x9, Pallas kernels: none -> 13.4 us  [the longest x1 4.37 us: body(): pl.pallas_call(weight_kernel, out_shape=(shape((112, 4096), BF),) * 2, in...]
    unnamed x4 -> x0, waiting for transfers between devices: 13 us -> none
  transfers between devices with their start and end apart: 5 -> 3, of which waited for: 4 -> 2; matrix products, arithmetic and copies ran while one was open for 6% -> 0% of each run, Pallas kernels for 0% -> 5%
where the time goes in v1:
time: 135 us; the launch traced here: 133 us
  blocking collectives  86.6 us (64%)
  starting transfers between devices  14.5 us (11%)
  Pallas kernels  13.4 us (10%)
  waiting for transfers between devices  13.1 us (10%)
  local copies, waits for them, and re-layouts  5.08 us (4%)
    all_to_all x1, blocking collectives, body(): lax.all_to_all(picked.reshape(DP * 4, ROWS, 128), FAR, 0, 0, tiled=True)  40.9 us
    all_to_all x1, blocking collectives, body(): mine = lax.all_to_all(spread, PLANE, 0, 0, tiled=True)  27.4 us
    all_to_all x1, blocking collectives, body(): parts = lax.all_to_all(summed, PLANE, 0, 0, tiled=True)  18.4 us
    all_to_all x1, waiting for transfers between devices, body(): lax.all_to_all(back.reshape(DP * 4, BACK, 128), FAR, 0, 0, tiled=True)  11 us
    ppermute x1, starting transfers between devices, body(): other = lax.ppermute(mine, 'core', swap)  6.43 us
    all_to_all x1, starting transfers between devices, body(): lax.all_to_all(back.reshape(DP * 4, BACK, 128), FAR, 0, 0, tiled=True)  6 us
    unnamed x16, local copies, waits for them, and re-layouts  5.08 us
    pallas_call x1, Pallas kernels, body(): pl.pallas_call(weight_kernel, out_shape=(shape((112, 4096), BF),) * 2, in...  4.37 us
  transfers between devices with their start and end apart: 3, of which 2 were waited for; matrix products, arithmetic and copies ran while one was open for 0% of the time, Pallas kernels for 5%

profile of v1, /device:TPU:1, one launch (start us, length us, event | category | flops | bytes accessed | tf_op | source)
XLA Modules:
  0.0 133.5 jit_solution(16417321930635369030)
XLA Ops:
  0.6 0.0 copy-start.3
  0.6 0.7 copy-done.3
  1.3 0.0 copy-start.4
  1.3 0.7 copy-done.4
  2.0 0.0 copy-start.5
  2.0 0.7 copy-done.5
  2.7 0.0 copy-start.7
  2.7 0.7 copy-done.7
  3.4 0.5 select_rows.1
  3.9 40.9 %all_to_all.20 = bf16[48,24,128]{2,1,0:T(8,128)(2,1)S(1)} all-to-all(bf16[48,24,128]{2,1,0:T(8,128)(2,1)S(1)} %bitcast.9), channel_id=1, replica_groups=mesh['dp'=12,'yh'=4,'yl'=2,'x'=4,'core'=2] {'dp','yh'}, dimensions={0} | all-to-all | bytes 589824 | tf_op jit(solution)/shard_map/all_to_all | solution.py:295
  44.8 0.6 spread_rows.1
  45.4 0.0 copy-start
  45.4 27.4 %all_to_all.21.mine = bf16[8,4,128,256]{3,2,1,0:T(8,128)(2,1)S(1)} all-to-all(bf16[8,4,128,256]{3,2,1,0:T(8,128)(2,1)S(1)} %get-tuple-element.16), channel_id=1, replica_groups=mesh['dp'=12,'yh'=4,'yl'=2,'x'=4,'core'=2] {'yl','x'}, dimensions={0} | all-to-all | bytes 4194304 | tf_op jit(solution)/shard_map/all_to_all | solution.py:309
  72.8 6.4 %collective-permute-start = (bf16[8,4,128,256]{3,2,1,0:T(8,128)(2,1)S(1)}, bf16[8,4,128,256]{3,2,1,0:T(8,128)(2,1)}, u32[]{:S(2)}, u32[]{:S(2)}) collective-permute-start(bf16[8,4,128,256]{3,2,1,0:T(8,128)(2,1)S(1)} %all_to_all.21.mine), channel_id=1, source_target_pairs={{0,1},{1,0},{2,3},{3,2},{4,5},{5,4},{6,7},{7,6},{8,9},{9,8},{10,11... | collective-permute-start | bytes 6291464 | tf_op jit(solution)/shard_map/ppermute | solution.py:311
  79.2 0.0 copy-done
  79.2 0.0 copy-start.1
  79.3 1.2 copy-done.1
  80.4 0.0 copy-start.2
  80.4 1.2 copy-done.2
  81.6 1.7 %own_features.1 = (bf16[336,2048]{1,0:T(8,128)(2,1)S(1)}, bf16[336,2048]{1,0:T(8,128)(2,1)S(1)}, f32[336,256]{1,0:T(8,128)S(1)}) custom-call(s32[1]{0:T(128)} %bitcast.1.core_ref, bf16[8,4,128,256]{3,2,1,0:T(8,128)(2,1)S(1)} %all_to_all.21.mine, bf16[112,4096]{1,0:T(8,128)(2,1)S(1)} %copy-done, bf16[112,4096]{1,0:T(8,128)(2,1)S(1)} %copy-done.1, ...), custom_call_target="tpu_custom_call" | custom-call | flops 360000000 | bytes 8000000 | tf_op jit(solution)/shard_map/own_features/pallas_call | solution.py:313
  83.3 0.0 collective-permute-done.other
  83.3 2.9 %hidden_and_input_grads.1 = (bf16[8,272,256]{2,1,0:T(8,128)(2,1)S(1)}, bf16[224,256]{1,0:T(8,128)(2,1)S(1)}, bf16[16,256]{1,0:T(8,128)(2,1)S(1)}) custom-call(bf16[8,4,128,256]{3,2,1,0:T(8,128)(2,1)} %collective-permute-done.other, f32[336,256]{1,0:T(8,128)S(1)} %get-tuple-element.18.part, f32[1,256]{1,0:T(1,128)S(1)} %get-tuple-element.19.prob, ...), custom_call_target="tpu_custom_call" | custom-call | flops 600000000 | bytes 5000000 | tf_op jit(solution)/shard_map/hidden_and_input_grads/pallas_call | solution.py:329
  86.2 2.1 %collective-permute-start.1 = (bf16[8,272,256]{2,1,0:T(8,128)(2,1)S(1)}, bf16[8,272,256]{2,1,0:T(8,128)(2,1)S(1)}, u32[]{:S(2)}, u32[]{:S(2)}) collective-permute-start(bf16[8,272,256]{2,1,0:T(8,128)(2,1)S(1)} %get-tuple-element.23), channel_id=1, source_target_pairs={{0,1},{1,0},{2,3},{3,2},{4,5},{5,4},{6,7},{7,6},{8,9},{9,8},{10,11... | collective-permute-start | bytes 3342344 | tf_op jit(solution)/shard_map/ppermute | solution.py:340
  88.3 0.5 input_grads_kept.1.keep
  88.8 2.0 %collective-permute-done.1.swapped = bf16[8,272,256]{2,1,0:T(8,128)(2,1)S(1)} collective-permute-done((bf16[8,272,256]{2,1,0:T(8,128)(2,1)S(1)}, bf16[8,272,256]{2,1,0:T(8,128)(2,1)S(1)}, u32[]{:S(2)}, u32[]{:S(2)}) %collective-permute-start.1) | collective-permute-done | bytes 1114144 | tf_op jit(solution)/shard_map/ppermute | solution.py:340
  90.8 0.4 add_cores.1
  91.2 18.4 %all_to_all.22.recv = bf16[8,272,256]{2,1,0:T(8,128)(2,1)S(1)} all-to-all(bf16[8,272,256]{2,1,0:T(8,128)(2,1)S(1)} %add_cores.1), channel_id=1, replica_groups=mesh['dp'=12,'yh'=4,'yl'=2,'x'=4,'core'=2] {'yl','x'}, dimensions={0} | all-to-all | bytes 2228224 | tf_op jit(solution)/shard_map/all_to_all | solution.py:378
  109.6 1.2 return_rows.1
  110.8 6.0 %all-to-all-start.3 = ((bf16[48,16,128]{2,1,0:T(8,128)(2,1)}), bf16[48,16,128]{2,1,0:T(8,128)(2,1)S(1)}, u32[]{:S(2)}, u32[]{:S(2)}) async-start(bf16[48,16,128]{2,1,0:T(8,128)(2,1)} %bitcast.5), calls=%async_computation.3 | async-start | bytes 393216 | tf_op jit(solution)/shard_map/all_to_all | solution.py:387
  116.8 0.0 copy-start.6
  116.8 4.4 %weight_grads.1 = (bf16[112,4096]{1,0:T(8,128)(2,1)}, bf16[112,4096]{1,0:T(8,128)(2,1)}) custom-call(s32[1]{0:T(128)} %bitcast.1.core_ref, bf16[8,4,128,256]{3,2,1,0:T(8,128)(2,1)S(1)} %all_to_all.21.mine, bf16[8,4,128,256]{3,2,1,0:T(8,128)(2,1)} %collective-permute-done.other, bf16[224,256]{1,0:T(8,128)(2,1)S(1)} %get-tuple-element.21.pre), custom_call_target="tpu_custom_call" | custom-call | flops 480000000 | bytes 4000000 | tf_op jit(solution)/shard_map/weight_grads/pallas_call | solution.py:352
  121.2 11.0 %all-to-all-done.3 = bf16[48,16,128]{2,1,0:T(8,128)(2,1)S(1)} async-done(((bf16[48,16,128]{2,1,0:T(8,128)(2,1)}), bf16[48,16,128]{2,1,0:T(8,128)(2,1)S(1)}, u32[]{:S(2)}, u32[]{:S(2)}) %all-to-all-start.3) | async-done | bytes 196640 | tf_op jit(solution)/shard_map/all_to_all | solution.py:387
  132.3 0.0 copy-done.6
  132.3 1.2 combine.1
Async XLA Ops:
  0.6 0.7 copy-start.3
  1.3 0.7 copy-start.4
  2.0 0.7 copy-start.5
  2.7 0.7 copy-start.7
  45.4 33.8 %copy-start = (bf16[112,4096]{1,0:T(8,128)(2,1)S(1)}, bf16[112,4096]{1,0:T(8,128)(2,1)}, u32[]{:S(2)}) copy-start(bf16[112,4096]{1,0:T(8,128)(2,1)} %wg.1) | copy-start | bytes 2752516
  72.8 10.5 %collective-permute-start = (bf16[8,4,128,256]{3,2,1,0:T(8,128)(2,1)S(1)}, bf16[8,4,128,256]{3,2,1,0:T(8,128)(2,1)}, u32[]{:S(2)}, u32[]{:S(2)}) collective-permute-start(bf16[8,4,128,256]{3,2,1,0:T(8,128)(2,1)S(1)} %all_to_all.21.mine), channel_id=1, source_target_pairs={{0,1},{1,0},{2,3},{3,2},{4,5},{5,4},{6,7},{7,6},{8,9},{9,8},{10,11... | collective-permute-start | bytes 6291464 | tf_op jit(solution)/shard_map/ppermute | solution.py:311
  79.2 1.2 copy-start.1
  80.4 1.2 copy-start.2
  86.2 4.6 %collective-permute-start.1 = (bf16[8,272,256]{2,1,0:T(8,128)(2,1)S(1)}, bf16[8,272,256]{2,1,0:T(8,128)(2,1)S(1)}, u32[]{:S(2)}, u32[]{:S(2)}) collective-permute-start(bf16[8,272,256]{2,1,0:T(8,128)(2,1)S(1)} %get-tuple-element.23), channel_id=1, source_target_pairs={{0,1},{1,0},{2,3},{3,2},{4,5},{5,4},{6,7},{7,6},{8,9},{9,8},{10,11... | collective-permute-start | bytes 3342344 | tf_op jit(solution)/shard_map/ppermute | solution.py:340
  110.8 21.4 %all-to-all-start.3 = ((bf16[48,16,128]{2,1,0:T(8,128)(2,1)}), bf16[48,16,128]{2,1,0:T(8,128)(2,1)S(1)}, u32[]{:S(2)}, u32[]{:S(2)}) async-start(bf16[48,16,128]{2,1,0:T(8,128)(2,1)} %bitcast.5), calls=%async_computation.3 | async-start | bytes 393216 | tf_op jit(solution)/shard_map/all_to_all | solution.py:387
  116.8 15.4 %copy-start.6 = (s32[32,2]{0,1:T(2,128)S(1)}, s32[32,2]{0,1:T(2,128)}, u32[]{:S(2)}) copy-start(s32[32,2]{0,1:T(2,128)} %param.9) | copy-start | bytes 772

commit v2 on v1

v2 whole, which is shorter than its diff:
```python
import jax
import jax.numpy as jnp
from jax import lax
from jax.experimental import pallas as pl
from jax.experimental.pallas import tpu as pltpu
from jax.sharding import Mesh, PartitionSpec as P

DP = 12
CAP = 20
SLOTS = 256
ROWS = 24
BACK = 16
BF = jnp.bfloat16
F32 = jnp.float32
VMEM = pl.BlockSpec(memory_space=pltpu.VMEM)
PLANE = ("yl", "x")
FAR = ("dp", "yh")


def iota(shape, dim):
    return lax.broadcasted_iota(jnp.int32, shape, dim)


def by24(r):
    return (r * 171) >> 12


def by20(s):
    return (s * 205) >> 12


def owner_of(j):
    return jnp.where(j < 8, j >> 2, j - 6)


def dot(a, b, ca, cb, precision=None):
    return lax.dot_general(
        a, b, (((ca,), (cb,)), ((), ())), preferred_element_type=F32, precision=precision
    )


def one_hot(mask):
    return jnp.where(mask, 1.0, 0.0)


def select_kernel(routes, probs, tokens, grads, out):
    rows = DP * ROWS
    r = iota((rows, 32), 0)
    j = by24(r)
    c = r - ROWS * j
    owner = owner_of(j)
    first = routes[0:1, :] == owner
    second = routes[1:2, :] == owner
    hit = one_hot(first | second)
    earlier = one_hot(iota((32, 32), 0) < iota((32, 32), 1)).astype(BF)
    rank = dot(hit.astype(BF), earlier, 1, 0)
    chosen = hit * one_hot(rank == c.astype(F32))
    p = probs[...].astype(F32)
    weight = jnp.sum(chosen * jnp.where(first, p[0:1, :], p[1:2, :]), axis=1, keepdims=True)
    values = jnp.concatenate([tokens[...].astype(F32), grads[...].astype(F32)], axis=1)
    picked = dot(chosen.astype(BF), values.astype(BF), 1, 0)
    rl = iota((rows, 128), 0)
    at_lane = one_hot(rl - ROWS * by24(rl) == iota((rows, 128), 1))
    ra, rb = iota((rows, rows), 0), iota((rows, rows), 1)
    ja = by24(ra)
    gather = one_hot((ra - ROWS * ja == CAP) & (ja == by24(rb)))
    picked += dot(gather.astype(BF), (weight * at_lane).astype(BF), 1, 0)
    block = picked.reshape(DP, ROWS, 128).astype(BF)
    for k in range(4):
        out[:, k] = block


def spread_kernel(recv, out, prob, held, sems):
    rows = DP * ROWS
    r, s = iota((rows, SLOTS), 0), iota((rows, SLOTS), 1)
    i = by20(s)
    used = s < DP * CAP
    place = one_hot((r == ROWS * i + (s - CAP * i)) & used).astype(BF)
    blocks = [recv[:, k].astype(F32).reshape(rows, 128).astype(BF) for k in range(4)]
    copies = []
    for k in range(4):
        held[k] = dot(blocks[k], place, 0, 0).astype(BF)
        for n in range(8):
            copy = pltpu.make_async_copy(held.at[k], out.at[n, k], sems.at[8 * k + n])
            copy.start()
            copies.append(copy)
    lane, sl = iota((128, SLOTS), 0), iota((128, SLOTS), 1)
    fan = one_hot(lane == sl - CAP * by20(sl)).astype(BF)
    fanned = dot(blocks[0], fan, 1, 0)
    prob[...] = jnp.sum(
        jnp.where((r == ROWS * i + CAP) & used, fanned, 0.0), axis=0, keepdims=True
    )
    for copy in copies:
        copy.wait()


def place_copies(core, mine, other, held, sems):
    copies = []
    for k in range(8):
        for n, src in enumerate((mine, other)):
            slot = core if n == 0 else 1 - core
            copies.append(
                pltpu.make_async_copy(
                    src.at[k, :, pl.ds(0, 64), :], held.at[:, k, slot], sems.at[2 * k + n]
                )
            )
    return copies


def split(v):
    high = v.astype(BF).astype(F32)
    return high, v - high


def two_rows(v):
    high, low = split(v)
    n = iota((16, SLOTS), 0)
    return jnp.where(n == 0, high, jnp.where(n == 1, low, 0.0)).astype(BF)


def sort_kernel(core_ref, wg, wu, wd, w_own, w_away, w, sems):
    core = core_ref[0]
    copies = []
    for n, src in enumerate((wg, wu, wd)):
        for q in range(4):
            at = pl.ds(1024 * q, 1024)
            dst = w.at[pl.ds(112 * n, 112), at]
            copies.append(pltpu.make_async_copy(src.at[:, at], dst, sems.at[4 * n + q]))
    for a in copies:
        a.start()
    for a in copies:
        a.wait()
    for k in range(8):
        blocks = [w[:, (yh * 8 + k) * 128 : (yh * 8 + k + 1) * 128] for yh in range(4)]
        low = jnp.concatenate([v[:, 0:64] for v in blocks], axis=1)
        high = jnp.concatenate([v[:, 64:128] for v in blocks], axis=1)
        at = pl.ds(256 * k, 256)
        w_own[:, at] = jnp.where(core == 0, low, high)
        w_away[:, at] = jnp.where(core == 0, high, low)


def hold_kernel(w, out):
    out[...] = w[...]


def features_kernel(mine, w, part):
    both = jnp.zeros((224, SLOTS), F32)
    back = jnp.zeros((112, SLOTS), F32)
    for k in range(8):
        at = pl.ds(256 * k, 256)
        both += dot(w[0:224, at], mine[k, :, 0:64, :].reshape(256, SLOTS), 1, 0)
        back += dot(w[224:336, at], mine[k, :, 64:128, :].reshape(256, SLOTS), 1, 0)
    part[0:224] = both
    part[224:336] = back


def hidden_kernel(own, got, prob, pre):
    gate = own[0:112] + got[0:112]
    up = own[112:224] + got[112:224]
    back = own[224:336] + got[224:336]
    sig = jax.nn.sigmoid(gate)
    silu = gate * sig
    scaled = prob[...] * back
    pre[0:112] = (scaled * up * sig * (1.0 + gate * (1.0 - sig))).astype(BF)
    pre[112:224] = (scaled * silu).astype(BF)
    pre[224:240] = two_rows(jnp.sum(silu * up * back, axis=0, keepdims=True))


def keep_kernel(w_own, pre, keep):
    for k in range(8):
        keep[k] = dot(w_own[0:224, pl.ds(256 * k, 256)], pre[0:224], 0, 0)


def sum_kernel(keep, w_near, pre, pre_near, out):
    terms = pre[224:240].astype(F32) + pre_near[224:240].astype(F32)
    router = two_rows(jnp.sum(terms, axis=0, keepdims=True))
    for k in range(8):
        part = dot(w_near[0:224, pl.ds(256 * k, 256)], pre_near[0:224], 0, 0)
        out[k, 0:256] = (keep[k] + part).astype(BF)
        out[k, 256:272] = router


def weight_kernel(core_ref, mine, other, pre, out_gate, out_up, done, xt, xsem):
    core = core_ref[0]
    copies = place_copies(core, mine, other, xt, xsem)
    for a in copies:
        a.start()
    for k in range(8):
        copies[2 * k].wait()
        copies[2 * k + 1].wait()
        part = dot(pre[0:224], xt[:, k].reshape(512, SLOTS), 1, 1).astype(BF)
        for yh in range(4):
            at = pl.ds((yh * 8 + k) * 128, 128)
            out_gate[:, at] = part[0:112, yh * 128 : (yh + 1) * 128]
            out_up[:, at] = part[112:224, yh * 128 : (yh + 1) * 128]
    done[...] = jnp.zeros((8, 128), F32)


def return_kernel(recv, out, held, sems):
    rows = DP * BACK
    total = recv[0, 0:256].astype(F32)
    terms = recv[0, 256:272].astype(F32)
    for k in range(1, 8):
        total += recv[k, 0:256].astype(F32)
        terms += recv[k, 256:272].astype(F32)
    high, low = split(jnp.sum(terms, axis=0, keepdims=True))
    r, s = iota((rows, SLOTS), 0), iota((rows, SLOTS), 1)
    i, c = r >> 4, r & 15
    in_block = (by20(s) == i) & (s < DP * CAP)
    slot = s - CAP * i
    left = one_hot(in_block & (slot == c) & (c < 10)).astype(BF)
    right = one_hot(in_block & (slot == c + 10) & (c < 10)).astype(BF)
    spread = jnp.where(in_block & (c == 10), high, jnp.where(in_block & (c == 11), low, 0.0))
    sl, lane = iota((SLOTS, 128), 0), iota((SLOTS, 128), 1)
    fan = one_hot(sl - CAP * by20(sl) == lane).astype(BF)
    terms_part = dot(spread.astype(BF), fan, 1, 0)
    empty = jnp.zeros((64, SLOTS), BF)
    copies = []
    for yh in range(4):
        block = total[yh * 64 : (yh + 1) * 64].astype(BF)
        part = terms_part + dot(left, jnp.concatenate([block, empty], axis=0), 1, 1)
        part += dot(right, jnp.concatenate([empty, block], axis=0), 1, 1)
        held[yh] = part.reshape(DP, BACK, 128).astype(BF)
        copies.append(pltpu.make_async_copy(held.at[yh], out.at[:, yh], sems.at[yh]))
        copies[yh].start()
    for copy in copies:
        copy.wait()


def mask_kernel(routes, after, chosen, masks):
    cols = DP * 4 * BACK
    eye = one_hot(iota((32, 32), 0) == iota((32, 32), 1))
    place = dot(eye.astype(BF), routes[...].astype(F32).astype(BF), 1, 1)
    first, second = place[:, 0:1], place[:, 1:2]
    r = iota((32, cols), 1)
    c = (r & 15).astype(F32)
    owner = owner_of(r >> 6).astype(F32)
    hit = one_hot((first == owner) | (second == owner))
    before = one_hot(iota((32, 32), 1) < iota((32, 32), 0)).astype(BF)
    rank = dot(before, hit.astype(BF), 1, 0)
    paired = hit * one_hot(c < 10.0)
    both = jnp.concatenate(
        [paired * one_hot(rank == c), paired * one_hot(rank == c + 10.0)], axis=0
    )
    chosen[...] = both.astype(BF)
    lane = iota((32, 128), 1).astype(F32)
    for j in range(DP):
        owner_j = float(j // 4 if j < 8 else j - 6)
        here = one_hot(rank[:, 64 * j : 64 * j + 1] == lane)
        masks[0, j] = jnp.where(first == owner_j, here, 0.0)
        masks[1, j] = jnp.where(second == owner_j, here, 0.0)


def combine_kernel(chosen, masks, recv, grad_tokens, grad_probs):
    both = dot(chosen[...], recv[...].reshape(DP * 4 * BACK, 128), 1, 0)
    grad_tokens[...] = (both[0:32, 0:64] + both[32:64, 64:128]).astype(BF)
    sums = [jnp.zeros((32, 128), F32), jnp.zeros((32, 128), F32)]
    for j in range(DP):
        terms = jnp.sum(recv[j].astype(F32), axis=0)
        term = terms[10:11] + terms[11:12]
        for n in range(2):
            sums[n] += jnp.where(masks[n, j] > 0.5, term, 0.0)
    ones = jnp.ones((8, 128), F32)
    for n in range(2):
        row = dot(ones, sums[n], 1, 1, lax.Precision.HIGHEST)
        grad_probs[n : n + 1, :] = row[0:1, :]


def params(mib=16):
    return pltpu.CompilerParams(vmem_limit_bytes=mib * 1024 * 1024)


def shape(dims, dtype):
    return jax.ShapeDtypeStruct(dims, dtype)


def body(tokens, grad_out, routes, probs, gate_weight, up_weight, down_weight):
    any_space = pl.BlockSpec(memory_space=pl.ANY)
    smem = pl.BlockSpec(memory_space=pltpu.SMEM)
    core = lax.axis_index("core").astype(jnp.int32).reshape(1)
    routes_t = routes.T
    whole = [pl.BlockSpec(dims, lambda n: (0, 0)) for dims in ((2, 32), (32, 64))]
    picked = pl.pallas_call(
        select_kernel,
        grid=(1,),
        out_shape=pltpu.VMEM((DP, 4, ROWS, 128), BF),
        in_specs=[whole[0], whole[0], whole[1], whole[1]],
        out_specs=pl.BlockSpec((DP, 4, ROWS, 128), lambda n: (0, 0, 0, 0)),
        compiler_params=params(60),
        name="select_rows",
    )(routes_t, probs.T, tokens, grad_out)
    swap = [(0, 1), (1, 0)]
    w_own, w_away = pl.pallas_call(
        sort_kernel,
        out_shape=(pltpu.VMEM((336, 2048), BF),) * 2,
        in_specs=[smem] + [pl.BlockSpec(memory_space=pltpu.HBM)] * 3,
        out_specs=(VMEM,) * 2,
        scratch_shapes=[pltpu.VMEM((336, 4096), BF), pltpu.SemaphoreType.DMA((12,))],
        compiler_params=params(),
        cost_estimate=pl.CostEstimate(
            flops=0, bytes_accessed=8_000_000, transcendentals=0
        ),
        name="sort_columns",
    )(core, gate_weight, up_weight, down_weight)
    w_near = pl.pallas_call(
        hold_kernel,
        out_shape=pltpu.VMEM((336, 2048), BF),
        in_specs=[VMEM],
        out_specs=VMEM,
        compiler_params=params(),
        name="hold_columns",
    )(lax.ppermute(w_away, "core", swap))
    got = lax.all_to_all(picked.reshape(DP * 4, ROWS, 128), FAR, 0, 0, tiled=True)
    spread, prob = pl.pallas_call(
        spread_kernel,
        out_shape=(pltpu.HBM((8, 4, 128, SLOTS), BF), shape((1, SLOTS), F32)),
        in_specs=[VMEM],
        out_specs=(any_space, VMEM),
        scratch_shapes=[pltpu.VMEM((4, 128, SLOTS), BF), pltpu.SemaphoreType.DMA((32,))],
        compiler_params=params(),
        name="spread_rows",
    )(got.reshape(DP, 4, ROWS, 128))
    mine = lax.all_to_all(spread, PLANE, 0, 0, tiled=True)
    away, part = [
        pl.pallas_call(
            features_kernel,
            out_shape=shape((336, SLOTS), F32),
            in_specs=[VMEM] * 2,
            out_specs=VMEM,
            compiler_params=params(),
            cost_estimate=pl.CostEstimate(
                flops=360_000_000, bytes_accessed=4_000_000, transcendentals=0
            ),
            name=name,
        )(mine, w)
        for name, w in (("features_away", w_near), ("features_own", w_own))
    ]
    got_part = lax.ppermute(away, "core", swap)
    pre = pl.pallas_call(
        hidden_kernel,
        out_shape=shape((240, SLOTS), BF),
        in_specs=[VMEM] * 3,
        out_specs=VMEM,
        compiler_params=params(),
        name="hidden_units",
    )(part, got_part, prob)
    pre_near = lax.ppermute(pre, "core", swap)
    keep = pl.pallas_call(
        keep_kernel,
        out_shape=shape((8, 256, SLOTS), F32),
        in_specs=[VMEM] * 2,
        out_specs=VMEM,
        compiler_params=params(),
        cost_estimate=pl.CostEstimate(
            flops=240_000_000, bytes_accessed=3_000_000, transcendentals=0
        ),
        name="input_grads_own",
    )(w_own, pre)
    summed = pl.pallas_call(
        sum_kernel,
        out_shape=shape((8, 272, SLOTS), BF),
        in_specs=[VMEM] * 4,
        out_specs=VMEM,
        compiler_params=params(),
        name="input_grads_both",
    )(keep, w_near, pre, pre_near)
    parts = lax.all_to_all(summed, PLANE, 0, 0, tiled=True)
    back = pl.pallas_call(
        return_kernel,
        out_shape=pltpu.HBM((DP, 4, BACK, 128), BF),
        in_specs=[VMEM],
        out_specs=any_space,
        scratch_shapes=[pltpu.VMEM((4, DP, BACK, 128), BF), pltpu.SemaphoreType.DMA((4,))],
        compiler_params=params(),
        name="return_rows",
    )(parts)
    late, back = lax.optimization_barrier((mine, back))
    other = lax.ppermute(late, "core", swap)
    grad_gate, grad_up, done = pl.pallas_call(
        weight_kernel,
        out_shape=(shape((112, 4096), BF),) * 2 + (shape((8, 128), F32),),
        in_specs=[smem, any_space, any_space, VMEM],
        out_specs=(VMEM,) * 3,
        scratch_shapes=[
            pltpu.VMEM((4, 8, 2, 64, SLOTS), BF),
            pltpu.SemaphoreType.DMA((16,)),
        ],
        compiler_params=params(),
        cost_estimate=pl.CostEstimate(
            flops=1_000, bytes_accessed=1_000, transcendentals=0
        ),
        name="weight_grads",
    )(core, late, other, pre)
    home = lax.all_to_all(back.reshape(DP * 4, BACK, 128), FAR, 0, 0, tiled=True)
    chosen, masks = pl.pallas_call(
        mask_kernel,
        out_shape=(shape((64, DP * 4 * BACK), BF), shape((2, DP, 32, 128), F32)),
        in_specs=[VMEM] * 2,
        out_specs=(VMEM,) * 2,
        compiler_params=params(),
        name="masks",
    )(routes_t, done)
    grad_tokens, grad_probs = pl.pallas_call(
        combine_kernel,
        out_shape=(shape((32, 64), BF), shape((2, 32), F32)),
        in_specs=[VMEM] * 3,
        out_specs=(VMEM,) * 2,
        compiler_params=params(),
        name="combine",
    )(chosen, masks, home.reshape(DP, 4, BACK, 128))
    return grad_tokens, grad_probs.T, grad_gate, grad_up


def solution(mesh):
    fine = Mesh(mesh.devices.reshape(DP, 4, 2, 4, 2), ("dp", "yh", "yl", "x", "core"))
    hidden = ("yh", "yl", "x", "core")
    rows = P(("dp",) + hidden, None)
    placed = (P("dp", hidden), P("dp", hidden), P("dp", None), P("dp", None), rows, rows, rows)
    return jax.shard_map(
        body,
        mesh=fine,
        in_specs=placed,
        out_specs=(P("dp", hidden), P("dp", None), rows, rows),
        check_vma=False,
    )
```

time: 135 us -> 131 us (0.970); the launches traced: 133 us -> 131 us
  blocking collectives: 86.6 us -> 59.8 us
  waiting for transfers between devices: 13.1 us -> 29.1 us
  starting transfers between devices: 14.5 us -> 23.5 us
  local copies, waits for them, and re-layouts: 5.08 us -> 3.46 us
    all_to_all x1 -> x0, blocking collectives: 27.4 us -> none  [body(): mine = lax.all_to_all(spread, PLANE, 0, 0, tiled=True)]
    all_to_all x0 -> x1, waiting for transfers between devices: none -> 13 us  [body(): mine = lax.all_to_all(spread, PLANE, 0, 0, tiled=True)]
    ppermute x2 -> x4, starting transfers between devices: 8.51 us -> 13.7 us  [the longest x1 4.85 us: body(): lax.ppermute(w_away, 'core', swap)]
    all_to_all x0 -> x1, starting transfers between devices: none -> 4.28 us  [body(): mine = lax.all_to_all(spread, PLANE, 0, 0, tiled=True)]
    ppermute x2 -> x4, waiting for transfers between devices: 2.05 us -> 3.87 us  [the longest x1 2.73 us: body(): lax.ppermute(w_away, 'core', swap)]
    unnamed x16, local copies, waits for them, and re-layouts: 5.08 us -> 3.46 us
    pallas_call x7 -> x11, Pallas kernels: 11.7 us -> 12.8 us  [the longest x1 4.37 us: body(): pl.pallas_call(weight_kernel, out_shape=(shape((112, 4096), BF),) * 2 + (...]
  transfers between devices with their start and end apart: 3 -> 6, of which waited for: 2 -> 5; matrix products, arithmetic and copies ran while one was open for 0% -> 0% of each run, Pallas kernels for 5% -> 6%
where the time goes in v2:
time: 131 us
  blocking collectives  59.8 us (46%)
  waiting for transfers between devices  29.1 us (22%)
  starting transfers between devices  23.5 us (18%)
  Pallas kernels  14.1 us (11%)
  local copies, waits for them, and re-layouts  3.46 us (3%)
    all_to_all x1, blocking collectives, body(): lax.all_to_all(picked.reshape(DP * 4, ROWS, 128), FAR, 0, 0, tiled=True)  40.9 us
    all_to_all x1, blocking collectives, body(): parts = lax.all_to_all(summed, PLANE, 0, 0, tiled=True)  18.9 us
    all_to_all x1, waiting for transfers between devices, body(): mine = lax.all_to_all(spread, PLANE, 0, 0, tiled=True)  13 us
    all_to_all x1, waiting for transfers between devices, body(): lax.all_to_all(back.reshape(DP * 4, BACK, 128), FAR, 0, 0, tiled=True)  12.3 us
    all_to_all x1, starting transfers between devices, body(): lax.all_to_all(back.reshape(DP * 4, BACK, 128), FAR, 0, 0, tiled=True)  5.53 us
    ppermute x1, starting transfers between devices, body(): lax.ppermute(w_away, 'core', swap)  4.85 us
    pallas_call x1, Pallas kernels, body(): pl.pallas_call(weight_kernel, out_shape=(shape((112, 4096), BF),) * 2 + (...  4.37 us
    all_to_all x1, starting transfers between devices, body(): mine = lax.all_to_all(spread, PLANE, 0, 0, tiled=True)  4.28 us
  transfers between devices with their start and end apart: 6, of which 5 were waited for; matrix products, arithmetic and copies ran while one was open for 0% of the time, Pallas kernels for 6%

profile of v2, /device:TPU:1, one launch (start us, length us, event | category | flops | bytes accessed | tf_op | source)
XLA Modules:
  0.0 130.9 jit_solution(13434665173187698109)
XLA Ops:
  0.6 1.2 select_rows.1
  1.9 40.9 %all_to_all.20 = bf16[48,24,128]{2,1,0:T(8,128)(2,1)S(1)} all-to-all(bf16[48,24,128]{2,1,0:T(8,128)(2,1)S(1)} %bitcast.9), channel_id=1, replica_groups=mesh['dp'=12,'yh'=4,'yl'=2,'x'=4,'core'=2] {'dp','yh'}, dimensions={0} | all-to-all | bytes 589824 | tf_op jit(solution)/shard_map/all_to_all | solution.py:313
  42.7 1.9 %spread_rows.1 = (bf16[8,4,128,256]{3,2,1,0:T(8,128)(2,1)}, f32[1,256]{1,0:T(1,128)S(1)}) custom-call(bf16[12,4,24,128]{3,2,1,0:T(8,128)(2,1)S(1)} %bitcast.8), custom_call_target="tpu_custom_call" | custom-call | tf_op jit(solution)/shard_map/spread_rows/pallas_call | solution.py:314
  44.6 0.0 copy-start.4
  44.7 4.3 %all-to-all-start.1 = ((bf16[8,4,128,256]{3,2,1,0:T(8,128)(2,1)}), bf16[8,4,128,256]{3,2,1,0:T(8,128)(2,1)S(1)}, u32[]{:S(2)}, u32[]{:S(2)}) async-start(bf16[8,4,128,256]{3,2,1,0:T(8,128)(2,1)} %get-tuple-element.17), calls=%async_computation.1 | async-start | bytes 4194304 | tf_op jit(solution)/shard_map/all_to_all | solution.py:323
  48.9 0.0 copy-done.4
  48.9 0.0 copy-start.5
  49.0 1.2 copy-done.5
  50.1 0.0 copy-start.6
  50.1 1.2 copy-done.6
  51.3 1.8 %sort_columns.1 = (bf16[336,2048]{1,0:T(8,128)(2,1)S(1)}, bf16[336,2048]{1,0:T(8,128)(2,1)S(1)}) custom-call(s32[1]{0:T(128)} %bitcast.1.core_ref, bf16[112,4096]{1,0:T(8,128)(2,1)S(1)} %copy-done.4, bf16[112,4096]{1,0:T(8,128)(2,1)S(1)} %copy-done.5, bf16[112,4096]{1,0:T(8,128)(2,1)S(1)} %copy-done.6), custom_call_target="tpu_custom_call" | custom-call | bytes 8000000 | tf_op jit(solution)/shard_map/sort_columns/pallas_call | solution.py:293
  53.1 0.0 copy-start
  53.1 1.1 copy-done
  54.2 4.9 %collective-permute-start = (bf16[336,2048]{1,0:T(8,128)(2,1)S(1)}, bf16[336,2048]{1,0:T(8,128)(2,1)S(1)}, u32[]{:S(2)}, u32[]{:S(2)}) collective-permute-start(bf16[336,2048]{1,0:T(8,128)(2,1)S(1)} %get-tuple-element.19), channel_id=1, source_target_pairs={{0,1},{1,0},{2,3},{3,2},{4,5},{5,4},{6,7},{7,6},{8,9},{9,8},{10,11... | collective-permute-start | bytes 4128776 | tf_op jit(solution)/shard_map/ppermute | solution.py:312
  59.0 2.7 %collective-permute-done.w = bf16[336,2048]{1,0:T(8,128)(2,1)S(1)} collective-permute-done((bf16[336,2048]{1,0:T(8,128)(2,1)S(1)}, bf16[336,2048]{1,0:T(8,128)(2,1)S(1)}, u32[]{:S(2)}, u32[]{:S(2)}) %collective-permute-start) | collective-permute-done | bytes 1376288 | tf_op jit(solution)/shard_map/ppermute | solution.py:312
  61.8 0.1 hold_columns.1.w.w_near
  61.9 13.0 %all-to-all-done.1.mine = bf16[8,4,128,256]{3,2,1,0:T(8,128)(2,1)S(1)} async-done(((bf16[8,4,128,256]{3,2,1,0:T(8,128)(2,1)}), bf16[8,4,128,256]{3,2,1,0:T(8,128)(2,1)S(1)}, u32[]{:S(2)}, u32[]{:S(2)}) %all-to-all-start.1) | async-done | bytes 2097184 | tf_op jit(solution)/shard_map/all_to_all | solution.py:323
  74.9 0.0 copy-start.1
  74.9 0.6 features_away.1
  75.4 3.0 %collective-permute-start.1 = (f32[336,256]{1,0:T(8,128)S(1)}, f32[336,256]{1,0:T(8,128)S(1)}, u32[]{:S(2)}, u32[]{:S(2)}) collective-permute-start(f32[336,256]{1,0:T(8,128)S(1)} %features_away.1), channel_id=1, source_target_pairs={{0,1},{1,0},{2,3},{3,2},{4,5},{5,4},{6,7},{7,6},{8,9},{9,8},{10,11... | collective-permute-start | bytes 1032200 | tf_op jit(solution)/shard_map/ppermute | solution.py:338
  78.4 0.0 copy-done.1
  78.4 0.6 features_own.1.own
  79.0 0.7 collective-permute-done.1.got
  79.7 0.1 hidden_units.1.pre
  79.8 0.0 copy-start.2
  79.8 2.3 %collective-permute-start.2 = (bf16[240,256]{1,0:T(8,128)(2,1)S(1)}, bf16[240,256]{1,0:T(8,128)(2,1)S(1)}, u32[]{:S(2)}, u32[]{:S(2)}) collective-permute-start(bf16[240,256]{1,0:T(8,128)(2,1)S(1)} %hidden_units.1.pre), channel_id=1, source_target_pairs={{0,1},{1,0},{2,3},{3,2},{4,5},{5,4},{6,7},{7,6},{8,9},{9,8},{10,11... | collective-permute-start | bytes 368648 | tf_op jit(solution)/shard_map/ppermute | solution.py:347
  82.1 0.5 input_grads_own.1.keep
  82.6 0.5 collective-permute-done.2.pre_near
  83.0 0.0 copy-done.2
  83.0 0.5 input_grads_both.1
  83.5 18.9 %all_to_all.21.recv = bf16[8,272,256]{2,1,0:T(8,128)(2,1)S(1)} all-to-all(bf16[8,272,256]{2,1,0:T(8,128)(2,1)S(1)} %input_grads_both.1), channel_id=1, replica_groups=mesh['dp'=12,'yh'=4,'yl'=2,'x'=4,'core'=2] {'yl','x'}, dimensions={0} | all-to-all | bytes 2228224 | tf_op jit(solution)/shard_map/all_to_all | solution.py:367
  102.5 0.0 copy-start.3
  102.5 1.2 return_rows.1
  103.7 3.6 %collective-permute-start.3 = (bf16[8,4,128,256]{3,2,1,0:T(8,128)(2,1)S(1)}, bf16[8,4,128,256]{3,2,1,0:T(8,128)(2,1)}, u32[]{:S(2)}, u32[]{:S(2)}) collective-permute-start(bf16[8,4,128,256]{3,2,1,0:T(8,128)(2,1)S(1)} %all-to-all-done.1.mine), channel_id=1, source_target_pairs={{0,1},{1,0},{2,3},{3,2},{4,5},{5,4},{6,7},{7,6},{8,9},{9,8},{10,11... | collective-permute-start | bytes 6291464 | tf_op jit(solution)/shard_map/ppermute | solution.py:378
  107.3 5.5 %all-to-all-start.3 = ((bf16[48,16,128]{2,1,0:T(8,128)(2,1)}), bf16[48,16,128]{2,1,0:T(8,128)(2,1)S(1)}, u32[]{:S(2)}, u32[]{:S(2)}) async-start(bf16[48,16,128]{2,1,0:T(8,128)(2,1)} %bitcast.13), calls=%async_computation.3 | async-start | bytes 393216 | tf_op jit(solution)/shard_map/all_to_all | solution.py:394
  112.9 0.0 copy-start.7
  112.9 0.0 collective-permute-done.3.other
  112.9 0.0 copy-done.3
  112.9 4.4 %weight_grads.1 = (bf16[112,4096]{1,0:T(8,128)(2,1)}, bf16[112,4096]{1,0:T(8,128)(2,1)}, f32[8,128]{1,0:T(8,128)S(1)}) custom-call(s32[1]{0:T(128)} %bitcast.1.core_ref, bf16[8,4,128,256]{3,2,1,0:T(8,128)(2,1)S(1)} %all-to-all-done.1.mine, bf16[8,4,128,256]{3,2,1,0:T(8,128)(2,1)} %collective-permute-done.3.other, bf16[240,256]{1,0:T(8,128)(2,1)S(1)} %copy-done.3), custom_call_target="tpu_custom_call" | custom-call | flops 1000 | bytes 1000 | tf_op jit(solution)/shard_map/weight_grads/pallas_call | solution.py:379
  117.3 0.0 copy-done.7
  117.3 0.5 masks.1
  117.8 12.3 %all-to-all-done.3 = bf16[48,16,128]{2,1,0:T(8,128)(2,1)S(1)} async-done(((bf16[48,16,128]{2,1,0:T(8,128)(2,1)}), bf16[48,16,128]{2,1,0:T(8,128)(2,1)S(1)}, u32[]{:S(2)}, u32[]{:S(2)}) %all-to-all-start.3) | async-done | bytes 196640 | tf_op jit(solution)/shard_map/all_to_all | solution.py:394
  130.0 0.8 combine.1
Async XLA Ops:
  44.6 4.3 %copy-start.4 = (bf16[112,4096]{1,0:T(8,128)(2,1)S(1)}, bf16[112,4096]{1,0:T(8,128)(2,1)}, u32[]{:S(2)}) copy-start(bf16[112,4096]{1,0:T(8,128)(2,1)} %wg.1) | copy-start | bytes 2752516
  44.7 30.2 %all-to-all-start.1 = ((bf16[8,4,128,256]{3,2,1,0:T(8,128)(2,1)}), bf16[8,4,128,256]{3,2,1,0:T(8,128)(2,1)S(1)}, u32[]{:S(2)}, u32[]{:S(2)}) async-start(bf16[8,4,128,256]{3,2,1,0:T(8,128)(2,1)} %get-tuple-element.17), calls=%async_computation.1 | async-start | bytes 4194304 | tf_op jit(solution)/shard_map/all_to_all | solution.py:323
  48.9 1.2 copy-start.5
  50.1 1.2 copy-start.6
  53.1 1.1 copy-start
  54.2 7.6 %collective-permute-start = (bf16[336,2048]{1,0:T(8,128)(2,1)S(1)}, bf16[336,2048]{1,0:T(8,128)(2,1)S(1)}, u32[]{:S(2)}, u32[]{:S(2)}) collective-permute-start(bf16[336,2048]{1,0:T(8,128)(2,1)S(1)} %get-tuple-element.19), channel_id=1, source_target_pairs={{0,1},{1,0},{2,3},{3,2},{4,5},{5,4},{6,7},{7,6},{8,9},{9,8},{10,11... | collective-permute-start | bytes 4128776 | tf_op jit(solution)/shard_map/ppermute | solution.py:312
  74.9 3.6 %copy-start.1 = (bf16[336,2048]{1,0:T(8,128)(2,1)S(1)}, bf16[336,2048]{1,0:T(8,128)(2,1)}, u32[]{:S(2)}) copy-start(bf16[336,2048]{1,0:T(8,128)(2,1)} %copy-done) | copy-start | bytes 4128772
  75.4 4.2 %collective-permute-start.1 = (f32[336,256]{1,0:T(8,128)S(1)}, f32[336,256]{1,0:T(8,128)S(1)}, u32[]{:S(2)}, u32[]{:S(2)}) collective-permute-start(f32[336,256]{1,0:T(8,128)S(1)} %features_away.1), channel_id=1, source_target_pairs={{0,1},{1,0},{2,3},{3,2},{4,5},{5,4},{6,7},{7,6},{8,9},{9,8},{10,11... | collective-permute-start | bytes 1032200 | tf_op jit(solution)/shard_map/ppermute | solution.py:338
  79.8 3.3 %copy-start.2 = (bf16[240,256]{1,0:T(8,128)(2,1)}, bf16[240,256]{1,0:T(8,128)(2,1)S(1)}, u32[]{:S(2)}) copy-start(bf16[240,256]{1,0:T(8,128)(2,1)S(1)} %hidden_units.1.pre) | copy-start | bytes 368644
  79.8 3.2 %collective-permute-start.2 = (bf16[240,256]{1,0:T(8,128)(2,1)S(1)}, bf16[240,256]{1,0:T(8,128)(2,1)S(1)}, u32[]{:S(2)}, u32[]{:S(2)}) collective-permute-start(bf16[240,256]{1,0:T(8,128)(2,1)S(1)} %hidden_units.1.pre), channel_id=1, source_target_pairs={{0,1},{1,0},{2,3},{3,2},{4,5},{5,4},{6,7},{7,6},{8,9},{9,8},{10,11... | collective-permute-start | bytes 368648 | tf_op jit(solution)/shard_map/ppermute | solution.py:347
  102.5 10.4 %copy-start.3 = (bf16[240,256]{1,0:T(8,128)(2,1)S(1)}, bf16[240,256]{1,0:T(8,128)(2,1)}, u32[]{:S(2)}) copy-start(bf16[240,256]{1,0:T(8,128)(2,1)} %copy-done.2) | copy-start | bytes 368644
  103.7 9.2 %collective-permute-start.3 = (bf16[8,4,128,256]{3,2,1,0:T(8,128)(2,1)S(1)}, bf16[8,4,128,256]{3,2,1,0:T(8,128)(2,1)}, u32[]{:S(2)}, u32[]{:S(2)}) collective-permute-start(bf16[8,4,128,256]{3,2,1,0:T(8,128)(2,1)S(1)} %all-to-all-done.1.mine), channel_id=1, source_target_pairs={{0,1},{1,0},{2,3},{3,2},{4,5},{5,4},{6,7},{7,6},{8,9},{9,8},{10,11... | collective-permute-start | bytes 6291464 | tf_op jit(solution)/shard_map/ppermute | solution.py:378
  107.3 22.7 %all-to-all-start.3 = ((bf16[48,16,128]{2,1,0:T(8,128)(2,1)}), bf16[48,16,128]{2,1,0:T(8,128)(2,1)S(1)}, u32[]{:S(2)}, u32[]{:S(2)}) async-start(bf16[48,16,128]{2,1,0:T(8,128)(2,1)} %bitcast.13), calls=%async_computation.3 | async-start | bytes 393216 | tf_op jit(solution)/shard_map/all_to_all | solution.py:394
  112.9 4.4 %copy-start.7 = (s32[32,2]{0,1:T(2,128)S(1)}, s32[32,2]{0,1:T(2,128)}, u32[]{:S(2)}) copy-start(s32[32,2]{0,1:T(2,128)} %param.9) | copy-start | bytes 772

commit v3 on v2

--- a/solution.py
+++ b/solution.py
@@ -171,13 +171,18 @@
         keep[k] = dot(w_own[0:224, pl.ds(256 * k, 256)], pre[0:224], 0, 0)
 
 
-def sum_kernel(keep, w_near, pre, pre_near, out):
+def sum_kernel(keep, w_near, pre, pre_near, out, held, sems):
     terms = pre[224:240].astype(F32) + pre_near[224:240].astype(F32)
     router = two_rows(jnp.sum(terms, axis=0, keepdims=True))
+    copies = []
     for k in range(8):
         part = dot(w_near[0:224, pl.ds(256 * k, 256)], pre_near[0:224], 0, 0)
-        out[k, 0:256] = (keep[k] + part).astype(BF)
-        out[k, 256:272] = router
+        held[k, 0:256] = (keep[k] + part).astype(BF)
+        held[k, 256:272] = router
+        copies.append(pltpu.make_async_copy(held.at[k], out.at[k], sems.at[k]))
+        copies[k].start()
+    for copy in copies:
+        copy.wait()
 
 
 def weight_kernel(core_ref, mine, other, pre, out_gate, out_up, done, xt, xsem):
@@ -358,9 +363,10 @@
     )(w_own, pre)
     summed = pl.pallas_call(
         sum_kernel,
-        out_shape=shape((8, 272, SLOTS), BF),
+        out_shape=pltpu.HBM((8, 272, SLOTS), BF),
         in_specs=[VMEM] * 4,
-        out_specs=VMEM,
+        out_specs=any_space,
+        scratch_shapes=[pltpu.VMEM((8, 272, SLOTS), BF), pltpu.SemaphoreType.DMA((8,))],
         compiler_params=params(),
         name="input_grads_both",
     )(keep, w_near, pre, pre_near)
@@ -374,8 +380,7 @@
         compiler_params=params(),
         name="return_rows",
     )(parts)
-    late, back = lax.optimization_barrier((mine, back))
-    other = lax.ppermute(late, "core", swap)
+    other = lax.ppermute(mine, "core", swap)
     grad_gate, grad_up, done = pl.pallas_call(
         weight_kernel,
         out_shape=(shape((112, 4096), BF),) * 2 + (shape((8, 128), F32),),
@@ -390,7 +395,7 @@
             flops=1_000, bytes_accessed=1_000, transcendentals=0
         ),
         name="weight_grads",
-    )(core, late, other, pre)
+    )(core, mine, other, pre)
     home = lax.all_to_all(back.reshape(DP * 4, BACK, 128), FAR, 0, 0, tiled=True)
     chosen, masks = pl.pallas_call(
         mask_kernel,

time: 131 us -> 129 us (0.985); the launches traced: 131 us -> 127 us
  blocking collectives: 59.8 us -> 40.9 us
  waiting for transfers between devices: 29.1 us -> 41.4 us
  starting transfers between devices: 23.5 us -> 26 us
    all_to_all x1 -> x0, blocking collectives: 18.9 us -> none  [body(): parts = lax.all_to_all(summed, PLANE, 0, 0, tiled=True)]
    all_to_all x0 -> x1, waiting for transfers between devices: none -> 13.1 us  [body(): parts = lax.all_to_all(summed, PLANE, 0, 0, tiled=True)]
    all_to_all x0 -> x1, starting transfers between devices: none -> 3.57 us  [body(): parts = lax.all_to_all(summed, PLANE, 0, 0, tiled=True)]
  transfers between devices with their start and end apart: 6 -> 7, of which waited for: 5 -> 6; matrix products, arithmetic and copies ran while one was open for 0% -> 0% of each run, Pallas kernels for 6% -> 7%
where the time goes in v3:
time: 129 us; the launch traced here: 127 us
  waiting for transfers between devices  41.4 us (32%)
  blocking collectives  40.9 us (32%)
  starting transfers between devices  26 us (20%)
  Pallas kernels  14.9 us (12%)
  local copies, waits for them, and re-layouts  3.48 us (3%)
    all_to_all x1, blocking collectives, body(): lax.all_to_all(picked.reshape(DP * 4, ROWS, 128), FAR, 0, 0, tiled=True)  40.9 us
    all_to_all x1, waiting for transfers between devices, body(): parts = lax.all_to_all(summed, PLANE, 0, 0, tiled=True)  13.1 us
    all_to_all x1, waiting for transfers between devices, body(): mine = lax.all_to_all(spread, PLANE, 0, 0, tiled=True)  13 us
    all_to_all x1, waiting for transfers between devices, body(): lax.all_to_all(back.reshape(DP * 4, BACK, 128), FAR, 0, 0, tiled=True)  11.4 us
    all_to_all x1, starting transfers between devices, body(): lax.all_to_all(back.reshape(DP * 4, BACK, 128), FAR, 0, 0, tiled=True)  5.53 us
    ppermute x1, starting transfers between devices, body(): lax.ppermute(w_away, 'core', swap)  4.85 us
    pallas_call x1, Pallas kernels, body(): pl.pallas_call(weight_kernel, out_shape=(shape((112, 4096), BF),) * 2 + (...  4.37 us
    all_to_all x1, starting transfers between devices, body(): mine = lax.all_to_all(spread, PLANE, 0, 0, tiled=True)  4.28 us
  transfers between devices with their start and end apart: 7, of which 6 were waited for; matrix products, arithmetic and copies ran while one was open for 0% of the time, Pallas kernels for 7%

profile of v3, /device:TPU:1, one launch (start us, length us, event | category | flops | bytes accessed | tf_op | source)
XLA Modules:
  0.0 127.4 jit_solution(9501915185086383804)
XLA Ops:
  0.6 1.2 select_rows.1
  1.9 40.9 %all_to_all.20 = bf16[48,24,128]{2,1,0:T(8,128)(2,1)S(1)} all-to-all(bf16[48,24,128]{2,1,0:T(8,128)(2,1)S(1)} %bitcast.9), channel_id=1, replica_groups=mesh['dp'=12,'yh'=4,'yl'=2,'x'=4,'core'=2] {'dp','yh'}, dimensions={0} | all-to-all | bytes 589824 | tf_op jit(solution)/shard_map/all_to_all | solution.py:318
  42.7 1.9 %spread_rows.1 = (bf16[8,4,128,256]{3,2,1,0:T(8,128)(2,1)}, f32[1,256]{1,0:T(1,128)S(1)}) custom-call(bf16[12,4,24,128]{3,2,1,0:T(8,128)(2,1)S(1)} %bitcast.8), custom_call_target="tpu_custom_call" | custom-call | tf_op jit(solution)/shard_map/spread_rows/pallas_call | solution.py:319
  44.6 0.0 copy-start.4
  44.6 4.3 %all-to-all-start.1 = ((bf16[8,4,128,256]{3,2,1,0:T(8,128)(2,1)}), bf16[8,4,128,256]{3,2,1,0:T(8,128)(2,1)S(1)}, u32[]{:S(2)}, u32[]{:S(2)}) async-start(bf16[8,4,128,256]{3,2,1,0:T(8,128)(2,1)} %get-tuple-element.15), calls=%async_computation.1 | async-start | bytes 4194304 | tf_op jit(solution)/shard_map/all_to_all | solution.py:328
  48.9 0.0 copy-done.4
  48.9 0.0 copy-start.5
  48.9 1.2 copy-done.5
  50.1 0.0 copy-start.6
  50.1 1.2 copy-done.6
  51.3 1.8 %sort_columns.1 = (bf16[336,2048]{1,0:T(8,128)(2,1)S(1)}, bf16[336,2048]{1,0:T(8,128)(2,1)S(1)}) custom-call(s32[1]{0:T(128)} %bitcast.1.core_ref, bf16[112,4096]{1,0:T(8,128)(2,1)S(1)} %copy-done.4, bf16[112,4096]{1,0:T(8,128)(2,1)S(1)} %copy-done.5, bf16[112,4096]{1,0:T(8,128)(2,1)S(1)} %copy-done.6), custom_call_target="tpu_custom_call" | custom-call | bytes 8000000 | tf_op jit(solution)/shard_map/sort_columns/pallas_call | solution.py:298
  53.0 0.0 copy-start
  53.0 1.1 copy-done
  54.1 4.9 %collective-permute-start.1 = (bf16[336,2048]{1,0:T(8,128)(2,1)S(1)}, bf16[336,2048]{1,0:T(8,128)(2,1)S(1)}, u32[]{:S(2)}, u32[]{:S(2)}) collective-permute-start(bf16[336,2048]{1,0:T(8,128)(2,1)S(1)} %get-tuple-element.17), channel_id=1, source_target_pairs={{0,1},{1,0},{2,3},{3,2},{4,5},{5,4},{6,7},{7,6},{8,9},{9,8},{10,11... | collective-permute-start | bytes 4128776 | tf_op jit(solution)/shard_map/ppermute | solution.py:317
  59.0 2.7 %collective-permute-done.1.w = bf16[336,2048]{1,0:T(8,128)(2,1)S(1)} collective-permute-done((bf16[336,2048]{1,0:T(8,128)(2,1)S(1)}, bf16[336,2048]{1,0:T(8,128)(2,1)S(1)}, u32[]{:S(2)}, u32[]{:S(2)}) %collective-permute-start.1) | collective-permute-done | bytes 1376288 | tf_op jit(solution)/shard_map/ppermute | solution.py:317
  61.7 0.1 hold_columns.1.w.w_near
  61.8 13.0 %all-to-all-done.1.mine = bf16[8,4,128,256]{3,2,1,0:T(8,128)(2,1)S(1)} async-done(((bf16[8,4,128,256]{3,2,1,0:T(8,128)(2,1)}), bf16[8,4,128,256]{3,2,1,0:T(8,128)(2,1)S(1)}, u32[]{:S(2)}, u32[]{:S(2)}) %all-to-all-start.1) | async-done | bytes 2097184 | tf_op jit(solution)/shard_map/all_to_all | solution.py:328
  74.8 0.0 copy-start.1
  74.8 0.6 features_away.1
  75.4 3.0 %collective-permute-start.2 = (f32[336,256]{1,0:T(8,128)S(1)}, f32[336,256]{1,0:T(8,128)S(1)}, u32[]{:S(2)}, u32[]{:S(2)}) collective-permute-start(f32[336,256]{1,0:T(8,128)S(1)} %features_away.1), channel_id=1, source_target_pairs={{0,1},{1,0},{2,3},{3,2},{4,5},{5,4},{6,7},{7,6},{8,9},{9,8},{10,11... | collective-permute-start | bytes 1032200 | tf_op jit(solution)/shard_map/ppermute | solution.py:343
  78.4 0.0 copy-done.1
  78.4 0.5 features_own.1.own
  78.9 0.7 collective-permute-done.2.got
  79.6 0.1 hidden_units.1.pre
  79.7 0.0 copy-start.2
  79.7 2.3 %collective-permute-start.3 = (bf16[240,256]{1,0:T(8,128)(2,1)S(1)}, bf16[240,256]{1,0:T(8,128)(2,1)S(1)}, u32[]{:S(2)}, u32[]{:S(2)}) collective-permute-start(bf16[240,256]{1,0:T(8,128)(2,1)S(1)} %hidden_units.1.pre), channel_id=1, source_target_pairs={{0,1},{1,0},{2,3},{3,2},{4,5},{5,4},{6,7},{7,6},{8,9},{9,8},{10,11... | collective-permute-start | bytes 368648 | tf_op jit(solution)/shard_map/ppermute | solution.py:352
  82.0 0.5 input_grads_own.1.keep
  82.5 0.5 collective-permute-done.3.pre_near
  83.0 0.0 copy-done.2
  83.0 1.4 %input_grads_both.1 = bf16[8,272,256]{2,1,0:T(8,128)(2,1)} custom-call(f32[8,256,256]{2,1,0:T(8,128)S(1)} %input_grads_own.1.keep, bf16[336,2048]{1,0:T(8,128)(2,1)S(1)} %hold_columns.1.w.w_near, bf16[240,256]{1,0:T(8,128)(2,1)S(1)} %hidden_units.1.pre, bf16[240,256]{1,0:T(8,128)(2,1)S(1)} %collective-permute-done.3.pre_near), custom_call_target="tpu_custom_call" | custom-call | tf_op jit(solution)/shard_map/input_grads_both/pallas_call | solution.py:364
  84.4 3.6 %all-to-all-start.2 = ((bf16[8,272,256]{2,1,0:T(8,128)(2,1)}), bf16[8,272,256]{2,1,0:T(8,128)(2,1)S(1)}, u32[]{:S(2)}, u32[]{:S(2)}) async-start(bf16[8,272,256]{2,1,0:T(8,128)(2,1)} %input_grads_both.1), calls=%async_computation.2 | async-start | bytes 2228224 | tf_op jit(solution)/shard_map/all_to_all | solution.py:373
  87.9 0.0 copy-start.3
  87.9 2.5 %collective-permute-start = (bf16[8,4,128,256]{3,2,1,0:T(8,128)(2,1)S(1)}, bf16[8,4,128,256]{3,2,1,0:T(8,128)(2,1)}, u32[]{:S(2)}, u32[]{:S(2)}) collective-permute-start(bf16[8,4,128,256]{3,2,1,0:T(8,128)(2,1)S(1)} %all-to-all-done.1.mine), channel_id=1, source_target_pairs={{0,1},{1,0},{2,3},{3,2},{4,5},{5,4},{6,7},{7,6},{8,9},{9,8},{10,11... | collective-permute-start | bytes 6291464 | tf_op jit(solution)/shard_map/ppermute | solution.py:383
  90.4 13.1 %all-to-all-done.2.recv = bf16[8,272,256]{2,1,0:T(8,128)(2,1)S(1)} async-done(((bf16[8,272,256]{2,1,0:T(8,128)(2,1)}), bf16[8,272,256]{2,1,0:T(8,128)(2,1)S(1)}, u32[]{:S(2)}, u32[]{:S(2)}) %all-to-all-start.2) | async-done | bytes 1114144 | tf_op jit(solution)/shard_map/all_to_all | solution.py:373
  103.5 1.2 return_rows.1
  104.8 5.5 %all-to-all-start.3 = ((bf16[48,16,128]{2,1,0:T(8,128)(2,1)}), bf16[48,16,128]{2,1,0:T(8,128)(2,1)S(1)}, u32[]{:S(2)}, u32[]{:S(2)}) async-start(bf16[48,16,128]{2,1,0:T(8,128)(2,1)} %bitcast.13), calls=%async_computation.3 | async-start | bytes 393216 | tf_op jit(solution)/shard_map/all_to_all | solution.py:399
  110.3 0.0 copy-start.7
  110.3 0.0 collective-permute-done.other
  110.3 0.0 copy-done.3
  110.3 4.4 %weight_grads.1 = (bf16[112,4096]{1,0:T(8,128)(2,1)}, bf16[112,4096]{1,0:T(8,128)(2,1)}, f32[8,128]{1,0:T(8,128)S(1)}) custom-call(s32[1]{0:T(128)} %bitcast.1.core_ref, bf16[8,4,128,256]{3,2,1,0:T(8,128)(2,1)S(1)} %all-to-all-done.1.mine, bf16[8,4,128,256]{3,2,1,0:T(8,128)(2,1)} %collective-permute-done.other, bf16[240,256]{1,0:T(8,128)(2,1)S(1)} %copy-done.3), custom_call_target="tpu_custom_call" | custom-call | flops 1000 | bytes 1000 | tf_op jit(solution)/shard_map/weight_grads/pallas_call | solution.py:384
  114.7 0.0 copy-done.7
  114.7 0.5 masks.1
  115.2 11.4 %all-to-all-done.3 = bf16[48,16,128]{2,1,0:T(8,128)(2,1)S(1)} async-done(((bf16[48,16,128]{2,1,0:T(8,128)(2,1)}), bf16[48,16,128]{2,1,0:T(8,128)(2,1)S(1)}, u32[]{:S(2)}, u32[]{:S(2)}) %all-to-all-start.3) | async-done | bytes 196640 | tf_op jit(solution)/shard_map/all_to_all | solution.py:399
  126.6 0.8 combine.1
Async XLA Ops:
  44.6 4.3 %copy-start.4 = (bf16[112,4096]{1,0:T(8,128)(2,1)S(1)}, bf16[112,4096]{1,0:T(8,128)(2,1)}, u32[]{:S(2)}) copy-start(bf16[112,4096]{1,0:T(8,128)(2,1)} %wg.1) | copy-start | bytes 2752516
  44.6 30.2 %all-to-all-start.1 = ((bf16[8,4,128,256]{3,2,1,0:T(8,128)(2,1)}), bf16[8,4,128,256]{3,2,1,0:T(8,128)(2,1)S(1)}, u32[]{:S(2)}, u32[]{:S(2)}) async-start(bf16[8,4,128,256]{3,2,1,0:T(8,128)(2,1)} %get-tuple-element.15), calls=%async_computation.1 | async-start | bytes 4194304 | tf_op jit(solution)/shard_map/all_to_all | solution.py:328
  48.9 1.2 copy-start.5
  50.1 1.2 copy-start.6
  53.0 1.1 copy-start
  54.1 7.6 %collective-permute-start.1 = (bf16[336,2048]{1,0:T(8,128)(2,1)S(1)}, bf16[336,2048]{1,0:T(8,128)(2,1)S(1)}, u32[]{:S(2)}, u32[]{:S(2)}) collective-permute-start(bf16[336,2048]{1,0:T(8,128)(2,1)S(1)} %get-tuple-element.17), channel_id=1, source_target_pairs={{0,1},{1,0},{2,3},{3,2},{4,5},{5,4},{6,7},{7,6},{8,9},{9,8},{10,11... | collective-permute-start | bytes 4128776 | tf_op jit(solution)/shard_map/ppermute | solution.py:317
  74.8 3.6 %copy-start.1 = (bf16[336,2048]{1,0:T(8,128)(2,1)S(1)}, bf16[336,2048]{1,0:T(8,128)(2,1)}, u32[]{:S(2)}) copy-start(bf16[336,2048]{1,0:T(8,128)(2,1)} %copy-done) | copy-start | bytes 4128772
  75.4 4.2 %collective-permute-start.2 = (f32[336,256]{1,0:T(8,128)S(1)}, f32[336,256]{1,0:T(8,128)S(1)}, u32[]{:S(2)}, u32[]{:S(2)}) collective-permute-start(f32[336,256]{1,0:T(8,128)S(1)} %features_away.1), channel_id=1, source_target_pairs={{0,1},{1,0},{2,3},{3,2},{4,5},{5,4},{6,7},{7,6},{8,9},{9,8},{10,11... | collective-permute-start | bytes 1032200 | tf_op jit(solution)/shard_map/ppermute | solution.py:343
  79.7 3.3 %copy-start.2 = (bf16[240,256]{1,0:T(8,128)(2,1)}, bf16[240,256]{1,0:T(8,128)(2,1)S(1)}, u32[]{:S(2)}) copy-start(bf16[240,256]{1,0:T(8,128)(2,1)S(1)} %hidden_units.1.pre) | copy-start | bytes 368644
  79.7 3.2 %collective-permute-start.3 = (bf16[240,256]{1,0:T(8,128)(2,1)S(1)}, bf16[240,256]{1,0:T(8,128)(2,1)S(1)}, u32[]{:S(2)}, u32[]{:S(2)}) collective-permute-start(bf16[240,256]{1,0:T(8,128)(2,1)S(1)} %hidden_units.1.pre), channel_id=1, source_target_pairs={{0,1},{1,0},{2,3},{3,2},{4,5},{5,4},{6,7},{7,6},{8,9},{9,8},{10,11... | collective-permute-start | bytes 368648 | tf_op jit(solution)/shard_map/ppermute | solution.py:352
  84.4 19.2 %all-to-all-start.2 = ((bf16[8,272,256]{2,1,0:T(8,128)(2,1)}), bf16[8,272,256]{2,1,0:T(8,128)(2,1)S(1)}, u32[]{:S(2)}, u32[]{:S(2)}) async-start(bf16[8,272,256]{2,1,0:T(8,128)(2,1)} %input_grads_both.1), calls=%async_computation.2 | async-start | bytes 2228224 | tf_op jit(solution)/shard_map/all_to_all | solution.py:373
  87.9 22.4 %copy-start.3 = (bf16[240,256]{1,0:T(8,128)(2,1)S(1)}, bf16[240,256]{1,0:T(8,128)(2,1)}, u32[]{:S(2)}) copy-start(bf16[240,256]{1,0:T(8,128)(2,1)} %copy-done.2) | copy-start | bytes 368644
  87.9 22.4 %collective-permute-start = (bf16[8,4,128,256]{3,2,1,0:T(8,128)(2,1)S(1)}, bf16[8,4,128,256]{3,2,1,0:T(8,128)(2,1)}, u32[]{:S(2)}, u32[]{:S(2)}) collective-permute-start(bf16[8,4,128,256]{3,2,1,0:T(8,128)(2,1)S(1)} %all-to-all-done.1.mine), channel_id=1, source_target_pairs={{0,1},{1,0},{2,3},{3,2},{4,5},{5,4},{6,7},{7,6},{8,9},{9,8},{10,11... | collective-permute-start | bytes 6291464 | tf_op jit(solution)/shard_map/ppermute | solution.py:383
  104.8 21.8 %all-to-all-start.3 = ((bf16[48,16,128]{2,1,0:T(8,128)(2,1)}), bf16[48,16,128]{2,1,0:T(8,128)(2,1)S(1)}, u32[]{:S(2)}, u32[]{:S(2)}) async-start(bf16[48,16,128]{2,1,0:T(8,128)(2,1)} %bitcast.13), calls=%async_computation.3 | async-start | bytes 393216 | tf_op jit(solution)/shard_map/all_to_all | solution.py:399
  110.3 4.4 %copy-start.7 = (s32[32,2]{0,1:T(2,128)S(1)}, s32[32,2]{0,1:T(2,128)}, u32[]{:S(2)}) copy-start(s32[32,2]{0,1:T(2,128)} %param.9) | copy-start | bytes 772

commit v4 on v3

--- a/solution.py
+++ b/solution.py
@@ -143,44 +143,52 @@
     out[...] = w[...]
 
 
-def features_kernel(mine, w, part):
+def add_features(mine, w, part, first):
     both = jnp.zeros((224, SLOTS), F32)
     back = jnp.zeros((112, SLOTS), F32)
     for k in range(8):
         at = pl.ds(256 * k, 256)
         both += dot(w[0:224, at], mine[k, :, 0:64, :].reshape(256, SLOTS), 1, 0)
         back += dot(w[224:336, at], mine[k, :, 64:128, :].reshape(256, SLOTS), 1, 0)
-    part[0:224] = both
-    part[224:336] = back
-
-
-def hidden_kernel(own, got, prob, pre):
-    gate = own[0:112] + got[0:112]
-    up = own[112:224] + got[112:224]
-    back = own[224:336] + got[224:336]
+    part[first : first + 224] = both
+    part[first + 224 : first + 336] = back
+
+
+def near_kernel(mine, w_near, part):
+    add_features(mine, w_near, part, 0)
+
+
+def own_kernel(mine, w_own, near, part):
+    part[0:336] = near[...]
+    add_features(mine, w_own, part, 336)
+
+
+def hidden_grads(v, prob):
+    gate, up, back = v[0:112], v[112:224], v[224:336]
     sig = jax.nn.sigmoid(gate)
     silu = gate * sig
-    scaled = prob[...] * back
-    pre[0:112] = (scaled * up * sig * (1.0 + gate * (1.0 - sig))).astype(BF)
-    pre[112:224] = (scaled * silu).astype(BF)
-    pre[224:240] = two_rows(jnp.sum(silu * up * back, axis=0, keepdims=True))
-
-
-def keep_kernel(w_own, pre, keep):
+    scaled = prob * back
+    d_gate = (scaled * up * sig * (1.0 + gate * (1.0 - sig))).astype(BF)
+    d_up = (scaled * silu).astype(BF)
+    router = jnp.sum(silu * up * back, axis=0, keepdims=True)
+    return jnp.concatenate([d_gate, d_up], axis=0), router
+
+
+def grads_kernel(part, got, prob, w_own, w_near, out, pre, held, own_held, sems):
+    own, own_terms = hidden_grads(part[336:672] + got[0:336], prob[...])
+    near, near_terms = hidden_grads(part[0:336] + got[336:672], prob[...])
+    own_held[...] = own
+    copies = [pltpu.make_async_copy(own_held, pre, sems.at[8])]
+    copies[0].start()
+    router = two_rows(own_terms + near_terms)
+    both = jnp.concatenate([own, near], axis=0)
     for k in range(8):
-        keep[k] = dot(w_own[0:224, pl.ds(256 * k, 256)], pre[0:224], 0, 0)
-
-
-def sum_kernel(keep, w_near, pre, pre_near, out, held, sems):
-    terms = pre[224:240].astype(F32) + pre_near[224:240].astype(F32)
-    router = two_rows(jnp.sum(terms, axis=0, keepdims=True))
-    copies = []
-    for k in range(8):
-        part = dot(w_near[0:224, pl.ds(256 * k, 256)], pre_near[0:224], 0, 0)
-        held[k, 0:256] = (keep[k] + part).astype(BF)
+        at = pl.ds(256 * k, 256)
+        w = jnp.concatenate([w_own[0:224, at], w_near[0:224, at]], axis=0)
+        held[k, 0:256] = dot(w, both, 0, 0).astype(BF)
         held[k, 256:272] = router
         copies.append(pltpu.make_async_copy(held.at[k], out.at[k], sems.at[k]))
-        copies[k].start()
+        copies[k + 1].start()
     for copy in copies:
         copy.wait()
 
@@ -193,7 +201,7 @@
     for k in range(8):
         copies[2 * k].wait()
         copies[2 * k + 1].wait()
-        part = dot(pre[0:224], xt[:, k].reshape(512, SLOTS), 1, 1).astype(BF)
+        part = dot(pre[...], xt[:, k].reshape(512, SLOTS), 1, 1).astype(BF)
         for yh in range(4):
             at = pl.ds((yh * 8 + k) * 128, 128)
             out_gate[:, at] = part[0:112, yh * 128 : (yh + 1) * 128]
@@ -326,50 +334,36 @@
         name="spread_rows",
     )(got.reshape(DP, 4, ROWS, 128))
     mine = lax.all_to_all(spread, PLANE, 0, 0, tiled=True)
-    away, part = [
-        pl.pallas_call(
-            features_kernel,
-            out_shape=shape((336, SLOTS), F32),
-            in_specs=[VMEM] * 2,
-            out_specs=VMEM,
-            compiler_params=params(),
-            cost_estimate=pl.CostEstimate(
-                flops=360_000_000, bytes_accessed=4_000_000, transcendentals=0
-            ),
-            name=name,
-        )(mine, w)
-        for name, w in (("features_away", w_near), ("features_own", w_own))
-    ]
-    got_part = lax.ppermute(away, "core", swap)
-    pre = pl.pallas_call(
-        hidden_kernel,
-        out_shape=shape((240, SLOTS), BF),
+    near = pl.pallas_call(
+        near_kernel,
+        out_shape=shape((336, SLOTS), F32),
+        in_specs=[VMEM] * 2,
+        out_specs=VMEM,
+        compiler_params=params(),
+        name="features_near",
+    )(mine, w_near)
+    part = pl.pallas_call(
+        own_kernel,
+        out_shape=shape((672, SLOTS), F32),
         in_specs=[VMEM] * 3,
         out_specs=VMEM,
         compiler_params=params(),
-        name="hidden_units",
-    )(part, got_part, prob)
-    pre_near = lax.ppermute(pre, "core", swap)
-    keep = pl.pallas_call(
-        keep_kernel,
-        out_shape=shape((8, 256, SLOTS), F32),
-        in_specs=[VMEM] * 2,
-        out_specs=VMEM,
-        compiler_params=params(),
-        cost_estimate=pl.CostEstimate(
-            flops=240_000_000, bytes_accessed=3_000_000, transcendentals=0
-        ),
-        name="input_grads_own",
-    )(w_own, pre)
-    summed = pl.pallas_call(
-        sum_kernel,
-        out_shape=pltpu.HBM((8, 272, SLOTS), BF),
-        in_specs=[VMEM] * 4,
-        out_specs=any_space,
-        scratch_shapes=[pltpu.VMEM((8, 272, SLOTS), BF), pltpu.SemaphoreType.DMA((8,))],
-        compiler_params=params(),
-        name="input_grads_both",
-    )(keep, w_near, pre, pre_near)
+        name="features_own",
+    )(mine, w_own, near)
+    got_part = lax.ppermute(part, "core", swap)
+    summed, pre = pl.pallas_call(
+        grads_kernel,
+        out_shape=(pltpu.HBM((8, 272, SLOTS), BF), pltpu.HBM((224, SLOTS), BF)),
+        in_specs=[VMEM] * 5,
+        out_specs=(any_space, any_space),
+        scratch_shapes=[
+            pltpu.VMEM((8, 272, SLOTS), BF),
+            pltpu.VMEM((224, SLOTS), BF),
+            pltpu.SemaphoreType.DMA((9,)),
+        ],
+        compiler_params=params(),
+        name="hidden_and_input_grads",
+    )(part, got_part, prob, w_own, w_near)
     parts = lax.all_to_all(summed, PLANE, 0, 0, tiled=True)
     back = pl.pallas_call(
         return_kernel,

time: 129 us -> 128 us (level)
  starting transfers between devices: 26 us -> 23.7 us
    ppermute x2 -> x1, starting transfers between devices: 5.26 us -> 2.99 us  [body(): got_part = lax.ppermute(part, 'core', swap)]
    unnamed x16 -> x14, local copies, waits for them, and re-layouts: 3.48 us -> 4.23 us
    pallas_call x5 -> x3, Pallas kernels: 3.05 us -> 2.79 us  [the longest x1 1.69 us: body(): pl.pallas_call(grads_kernel, out_shape=(pltpu.HBM((8, 272, SLOTS), BF), p...]
  transfers between devices with their start and end apart: 7 -> 6, of which waited for: 6 -> 5; matrix products, arithmetic and copies ran while one was open for 0% -> 0% of each run, Pallas kernels for 7% -> 6%
where the time goes in v4:
time: 128 us; the launch traced here: 126 us
  waiting for transfers between devices  42 us (33%)
  blocking collectives  40.9 us (32%)
  starting transfers between devices  23.7 us (19%)
  Pallas kernels  14.6 us (11%)
  local copies, waits for them, and re-layouts  4.23 us (3%)
    all_to_all x1, blocking collectives, body(): lax.all_to_all(picked.reshape(DP * 4, ROWS, 128), FAR, 0, 0, tiled=True)  40.9 us
    all_to_all x1, waiting for transfers between devices, body(): parts = lax.all_to_all(summed, PLANE, 0, 0, tiled=True)  13.1 us
    all_to_all x1, waiting for transfers between devices, body(): mine = lax.all_to_all(spread, PLANE, 0, 0, tiled=True)  13 us
    all_to_all x1, waiting for transfers between devices, body(): lax.all_to_all(back.reshape(DP * 4, BACK, 128), FAR, 0, 0, tiled=True)  11.4 us
    all_to_all x1, starting transfers between devices, body(): lax.all_to_all(back.reshape(DP * 4, BACK, 128), FAR, 0, 0, tiled=True)  5.52 us
    ppermute x1, starting transfers between devices, body(): lax.ppermute(w_away, 'core', swap)  4.85 us
    pallas_call x1, Pallas kernels, body(): pl.pallas_call(weight_kernel, out_shape=(shape((112, 4096), BF),) * 2 + (...  4.37 us
    all_to_all x1, starting transfers between devices, body(): mine = lax.all_to_all(spread, PLANE, 0, 0, tiled=True)  4.28 us
  transfers between devices with their start and end apart: 6, of which 5 were waited for; matrix products, arithmetic and copies ran while one was open for 0% of the time, Pallas kernels for 6%

profile of v4, /device:TPU:1, one launch (start us, length us, event | category | flops | bytes accessed | tf_op | source)
XLA Modules:
  0.0 126.2 jit_solution(15453926359352411457)
XLA Ops:
  0.6 1.2 select_rows.1
  1.9 40.9 %all_to_all.20 = bf16[48,24,128]{2,1,0:T(8,128)(2,1)S(1)} all-to-all(bf16[48,24,128]{2,1,0:T(8,128)(2,1)S(1)} %bitcast.9), channel_id=1, replica_groups=mesh['dp'=12,'yh'=4,'yl'=2,'x'=4,'core'=2] {'dp','yh'}, dimensions={0} | all-to-all | bytes 589824 | tf_op jit(solution)/shard_map/all_to_all | solution.py:326
  42.7 1.8 %spread_rows.1 = (bf16[8,4,128,256]{3,2,1,0:T(8,128)(2,1)}, f32[1,256]{1,0:T(1,128)S(1)}) custom-call(bf16[12,4,24,128]{3,2,1,0:T(8,128)(2,1)S(1)} %bitcast.8), custom_call_target="tpu_custom_call" | custom-call | tf_op jit(solution)/shard_map/spread_rows/pallas_call | solution.py:327
  44.6 0.0 copy-start.2
  44.6 4.3 %all-to-all-start.1 = ((bf16[8,4,128,256]{3,2,1,0:T(8,128)(2,1)}), bf16[8,4,128,256]{3,2,1,0:T(8,128)(2,1)S(1)}, u32[]{:S(2)}, u32[]{:S(2)}) async-start(bf16[8,4,128,256]{3,2,1,0:T(8,128)(2,1)} %get-tuple-element.17), calls=%async_computation.1 | async-start | bytes 4194304 | tf_op jit(solution)/shard_map/all_to_all | solution.py:336
  48.9 0.0 copy-done.2
  48.9 0.0 copy-start.3
  48.9 1.2 copy-done.3
  50.1 0.0 copy-start.4
  50.1 1.2 copy-done.4
  51.3 1.8 %sort_columns.1 = (bf16[336,2048]{1,0:T(8,128)(2,1)S(1)}, bf16[336,2048]{1,0:T(8,128)(2,1)S(1)}) custom-call(s32[1]{0:T(128)} %bitcast.1.core_ref, bf16[112,4096]{1,0:T(8,128)(2,1)S(1)} %copy-done.2, bf16[112,4096]{1,0:T(8,128)(2,1)S(1)} %copy-done.3, bf16[112,4096]{1,0:T(8,128)(2,1)S(1)} %copy-done.4), custom_call_target="tpu_custom_call" | custom-call | bytes 8000000 | tf_op jit(solution)/shard_map/sort_columns/pallas_call | solution.py:306
  53.0 0.0 copy-start
  53.0 1.1 copy-done
  54.1 4.9 %collective-permute-start.1 = (bf16[336,2048]{1,0:T(8,128)(2,1)S(1)}, bf16[336,2048]{1,0:T(8,128)(2,1)S(1)}, u32[]{:S(2)}, u32[]{:S(2)}) collective-permute-start(bf16[336,2048]{1,0:T(8,128)(2,1)S(1)} %get-tuple-element.19), channel_id=1, source_target_pairs={{0,1},{1,0},{2,3},{3,2},{4,5},{5,4},{6,7},{7,6},{8,9},{9,8},{10,11... | collective-permute-start | bytes 4128776 | tf_op jit(solution)/shard_map/ppermute | solution.py:325
  59.0 2.7 %collective-permute-done.1.w = bf16[336,2048]{1,0:T(8,128)(2,1)S(1)} collective-permute-done((bf16[336,2048]{1,0:T(8,128)(2,1)S(1)}, bf16[336,2048]{1,0:T(8,128)(2,1)S(1)}, u32[]{:S(2)}, u32[]{:S(2)}) %collective-permute-start.1) | collective-permute-done | bytes 1376288 | tf_op jit(solution)/shard_map/ppermute | solution.py:325
  61.7 0.1 hold_columns.1.w_near
  61.8 13.0 %all-to-all-done.1.mine = bf16[8,4,128,256]{3,2,1,0:T(8,128)(2,1)S(1)} async-done(((bf16[8,4,128,256]{3,2,1,0:T(8,128)(2,1)}), bf16[8,4,128,256]{3,2,1,0:T(8,128)(2,1)S(1)}, u32[]{:S(2)}, u32[]{:S(2)}) %all-to-all-start.1) | async-done | bytes 2097184 | tf_op jit(solution)/shard_map/all_to_all | solution.py:336
  74.8 0.0 copy-start.1
  74.8 0.6 features_near.1.near
  75.4 0.8 copy-done.1
  76.1 0.5 features_own.1.part
  76.7 3.0 %collective-permute-start.2 = (f32[672,256]{1,0:T(8,128)S(1)}, f32[672,256]{1,0:T(8,128)S(1)}, u32[]{:S(2)}, u32[]{:S(2)}) collective-permute-start(f32[672,256]{1,0:T(8,128)S(1)} %features_own.1.part), channel_id=1, source_target_pairs={{0,1},{1,0},{2,3},{3,2},{4,5},{5,4},{6,7},{7,6},{8,9},{9,8},{10,11... | collective-permute-start | bytes 2064392 | tf_op jit(solution)/shard_map/ppermute | solution.py:353
  79.7 1.7 %collective-permute-done.2.got = f32[672,256]{1,0:T(8,128)S(1)} collective-permute-done((f32[672,256]{1,0:T(8,128)S(1)}, f32[672,256]{1,0:T(8,128)S(1)}, u32[]{:S(2)}, u32[]{:S(2)}) %collective-permute-start.2) | collective-permute-done | bytes 688160 | tf_op jit(solution)/shard_map/ppermute | solution.py:353
  81.4 1.7 %hidden_and_input_grads.1 = (bf16[8,272,256]{2,1,0:T(8,128)(2,1)}, bf16[224,256]{1,0:T(8,128)(2,1)}) custom-call(f32[672,256]{1,0:T(8,128)S(1)} %features_own.1.part, f32[672,256]{1,0:T(8,128)S(1)} %collective-permute-done.2.got, f32[1,256]{1,0:T(1,128)S(1)} %get-tuple-element.20.prob, bf16[336,2048]{1,0:T(8,128)(2,1)S(1)} %copy-done.1, ...), custom_call_target="tpu_custom_call" | custom-call | tf_op jit(solution)/shard_map/hidden_and_input_grads/pallas_call | solution.py:354
  83.1 3.6 %all-to-all-start.2 = ((bf16[8,272,256]{2,1,0:T(8,128)(2,1)}), bf16[8,272,256]{2,1,0:T(8,128)(2,1)S(1)}, u32[]{:S(2)}, u32[]{:S(2)}) async-start(bf16[8,272,256]{2,1,0:T(8,128)(2,1)} %get-tuple-element.25), calls=%async_computation.2 | async-start | bytes 2228224 | tf_op jit(solution)/shard_map/all_to_all | solution.py:367
  86.7 0.0 copy-start.5
  86.7 2.5 %collective-permute-start = (bf16[8,4,128,256]{3,2,1,0:T(8,128)(2,1)S(1)}, bf16[8,4,128,256]{3,2,1,0:T(8,128)(2,1)}, u32[]{:S(2)}, u32[]{:S(2)}) collective-permute-start(bf16[8,4,128,256]{3,2,1,0:T(8,128)(2,1)S(1)} %all-to-all-done.1.mine), channel_id=1, source_target_pairs={{0,1},{1,0},{2,3},{3,2},{4,5},{5,4},{6,7},{7,6},{8,9},{9,8},{10,11... | collective-permute-start | bytes 6291464 | tf_op jit(solution)/shard_map/ppermute | solution.py:377
  89.2 13.1 %all-to-all-done.2.recv = bf16[8,272,256]{2,1,0:T(8,128)(2,1)S(1)} async-done(((bf16[8,272,256]{2,1,0:T(8,128)(2,1)}), bf16[8,272,256]{2,1,0:T(8,128)(2,1)S(1)}, u32[]{:S(2)}, u32[]{:S(2)}) %all-to-all-start.2) | async-done | bytes 1114144 | tf_op jit(solution)/shard_map/all_to_all | solution.py:367
  102.3 1.2 return_rows.1
  103.5 5.5 %all-to-all-start.3 = ((bf16[48,16,128]{2,1,0:T(8,128)(2,1)}), bf16[48,16,128]{2,1,0:T(8,128)(2,1)S(1)}, u32[]{:S(2)}, u32[]{:S(2)}) async-start(bf16[48,16,128]{2,1,0:T(8,128)(2,1)} %bitcast.13), calls=%async_computation.3 | async-start | bytes 393216 | tf_op jit(solution)/shard_map/all_to_all | solution.py:393
  109.1 0.0 collective-permute-done.other
  109.1 0.0 copy-done.5
  109.1 0.0 copy-start.6
  109.1 4.4 %weight_grads.1 = (bf16[112,4096]{1,0:T(8,128)(2,1)}, bf16[112,4096]{1,0:T(8,128)(2,1)}, f32[8,128]{1,0:T(8,128)S(1)}) custom-call(s32[1]{0:T(128)} %bitcast.1.core_ref, bf16[8,4,128,256]{3,2,1,0:T(8,128)(2,1)S(1)} %all-to-all-done.1.mine, bf16[8,4,128,256]{3,2,1,0:T(8,128)(2,1)} %collective-permute-done.other, bf16[224,256]{1,0:T(8,128)(2,1)S(1)} %copy-done.5), custom_call_target="tpu_custom_call" | custom-call | flops 1000 | bytes 1000 | tf_op jit(solution)/shard_map/weight_grads/pallas_call | solution.py:378
  113.5 0.0 copy-done.6
  113.5 0.5 masks.1
  114.0 11.4 %all-to-all-done.3 = bf16[48,16,128]{2,1,0:T(8,128)(2,1)S(1)} async-done(((bf16[48,16,128]{2,1,0:T(8,128)(2,1)}), bf16[48,16,128]{2,1,0:T(8,128)(2,1)S(1)}, u32[]{:S(2)}, u32[]{:S(2)}) %all-to-all-start.3) | async-done | bytes 196640 | tf_op jit(solution)/shard_map/all_to_all | solution.py:393
  125.4 0.8 combine.1
Async XLA Ops:
  44.6 4.3 %copy-start.2 = (bf16[112,4096]{1,0:T(8,128)(2,1)S(1)}, bf16[112,4096]{1,0:T(8,128)(2,1)}, u32[]{:S(2)}) copy-start(bf16[112,4096]{1,0:T(8,128)(2,1)} %wg.1) | copy-start | bytes 2752516
  44.6 30.2 %all-to-all-start.1 = ((bf16[8,4,128,256]{3,2,1,0:T(8,128)(2,1)}), bf16[8,4,128,256]{3,2,1,0:T(8,128)(2,1)S(1)}, u32[]{:S(2)}, u32[]{:S(2)}) async-start(bf16[8,4,128,256]{3,2,1,0:T(8,128)(2,1)} %get-tuple-element.17), calls=%async_computation.1 | async-start | bytes 4194304 | tf_op jit(solution)/shard_map/all_to_all | solution.py:336
  48.9 1.2 copy-start.3
  50.1 1.2 copy-start.4
  53.0 1.1 copy-start
  54.1 7.6 %collective-permute-start.1 = (bf16[336,2048]{1,0:T(8,128)(2,1)S(1)}, bf16[336,2048]{1,0:T(8,128)(2,1)S(1)}, u32[]{:S(2)}, u32[]{:S(2)}) collective-permute-start(bf16[336,2048]{1,0:T(8,128)(2,1)S(1)} %get-tuple-element.19), channel_id=1, source_target_pairs={{0,1},{1,0},{2,3},{3,2},{4,5},{5,4},{6,7},{7,6},{8,9},{9,8},{10,11... | collective-permute-start | bytes 4128776 | tf_op jit(solution)/shard_map/ppermute | solution.py:325
  74.8 1.3 %copy-start.1 = (bf16[336,2048]{1,0:T(8,128)(2,1)S(1)}, bf16[336,2048]{1,0:T(8,128)(2,1)}, u32[]{:S(2)}) copy-start(bf16[336,2048]{1,0:T(8,128)(2,1)} %copy-done) | copy-start | bytes 4128772
  76.7 4.7 %collective-permute-start.2 = (f32[672,256]{1,0:T(8,128)S(1)}, f32[672,256]{1,0:T(8,128)S(1)}, u32[]{:S(2)}, u32[]{:S(2)}) collective-permute-start(f32[672,256]{1,0:T(8,128)S(1)} %features_own.1.part), channel_id=1, source_target_pairs={{0,1},{1,0},{2,3},{3,2},{4,5},{5,4},{6,7},{7,6},{8,9},{9,8},{10,11... | collective-permute-start | bytes 2064392 | tf_op jit(solution)/shard_map/ppermute | solution.py:353
  83.1 19.2 %all-to-all-start.2 = ((bf16[8,272,256]{2,1,0:T(8,128)(2,1)}), bf16[8,272,256]{2,1,0:T(8,128)(2,1)S(1)}, u32[]{:S(2)}, u32[]{:S(2)}) async-start(bf16[8,272,256]{2,1,0:T(8,128)(2,1)} %get-tuple-element.25), calls=%async_computation.2 | async-start | bytes 2228224 | tf_op jit(solution)/shard_map/all_to_all | solution.py:367
  86.7 22.4 %copy-start.5 = (bf16[224,256]{1,0:T(8,128)(2,1)S(1)}, bf16[224,256]{1,0:T(8,128)(2,1)}, u32[]{:S(2)}) copy-start(bf16[224,256]{1,0:T(8,128)(2,1)} %get-tuple-element.21.pre) | copy-start | bytes 344068
  86.7 22.4 %collective-permute-start = (bf16[8,4,128,256]{3,2,1,0:T(8,128)(2,1)S(1)}, bf16[8,4,128,256]{3,2,1,0:T(8,128)(2,1)}, u32[]{:S(2)}, u32[]{:S(2)}) collective-permute-start(bf16[8,4,128,256]{3,2,1,0:T(8,128)(2,1)S(1)} %all-to-all-done.1.mine), channel_id=1, source_target_pairs={{0,1},{1,0},{2,3},{3,2},{4,5},{5,4},{6,7},{7,6},{8,9},{9,8},{10,11... | collective-permute-start | bytes 6291464 | tf_op jit(solution)/shard_map/ppermute | solution.py:377
  103.5 21.8 %all-to-all-start.3 = ((bf16[48,16,128]{2,1,0:T(8,128)(2,1)}), bf16[48,16,128]{2,1,0:T(8,128)(2,1)S(1)}, u32[]{:S(2)}, u32[]{:S(2)}) async-start(bf16[48,16,128]{2,1,0:T(8,128)(2,1)} %bitcast.13), calls=%async_computation.3 | async-start | bytes 393216 | tf_op jit(solution)/shard_map/all_to_all | solution.py:393
  109.1 4.4 %copy-start.6 = (s32[32,2]{0,1:T(2,128)S(1)}, s32[32,2]{0,1:T(2,128)}, u32[]{:S(2)}) copy-start(s32[32,2]{0,1:T(2,128)} %param.9) | copy-start | bytes 772

commit v5 on v4

--- a/solution.py
+++ b/solution.py
@@ -61,11 +61,9 @@
     picked = dot(chosen.astype(BF), values.astype(BF), 1, 0)
     rl = iota((rows, 128), 0)
     at_lane = one_hot(rl - ROWS * by24(rl) == iota((rows, 128), 1))
-    ra, rb = iota((rows, rows), 0), iota((rows, rows), 1)
-    ja = by24(ra)
-    gather = one_hot((ra - ROWS * ja == CAP) & (ja == by24(rb)))
-    picked += dot(gather.astype(BF), (weight * at_lane).astype(BF), 1, 0)
-    block = picked.reshape(DP, ROWS, 128).astype(BF)
+    weights = jnp.sum((weight * at_lane).reshape(DP, ROWS, 128), axis=1, keepdims=True)
+    last = iota((DP, ROWS, 128), 1) == CAP
+    block = (picked.reshape(DP, ROWS, 128) + jnp.where(last, weights, 0.0)).astype(BF)
     for k in range(4):
         out[:, k] = block
 
@@ -76,17 +74,17 @@
     i = by20(s)
     used = s < DP * CAP
     place = one_hot((r == ROWS * i + (s - CAP * i)) & used).astype(BF)
-    blocks = [recv[:, k].astype(F32).reshape(rows, 128).astype(BF) for k in range(4)]
     copies = []
     for k in range(4):
-        held[k] = dot(blocks[k], place, 0, 0).astype(BF)
+        block = recv[:, k].astype(F32).reshape(rows, 128).astype(BF)
+        held[k] = dot(block, place, 0, 0).astype(BF)
         for n in range(8):
             copy = pltpu.make_async_copy(held.at[k], out.at[n, k], sems.at[8 * k + n])
             copy.start()
             copies.append(copy)
     lane, sl = iota((128, SLOTS), 0), iota((128, SLOTS), 1)
     fan = one_hot(lane == sl - CAP * by20(sl)).astype(BF)
-    fanned = dot(blocks[0], fan, 1, 0)
+    fanned = dot(block, fan, 1, 0)
     prob[...] = jnp.sum(
         jnp.where((r == ROWS * i + CAP) & used, fanned, 0.0), axis=0, keepdims=True
     )

time: 128 us -> 128 us (level)
  no operation moved by 1% of the time
where the time goes in v5:
time: 128 us; the launch traced here: 126 us
  waiting for transfers between devices  42 us (33%)
  blocking collectives  40.9 us (32%)
  starting transfers between devices  23.7 us (19%)
  Pallas kernels  14.4 us (11%)
  local copies, waits for them, and re-layouts  4.24 us (3%)
    all_to_all x1, blocking collectives, body(): lax.all_to_all(picked.reshape(DP * 4, ROWS, 128), FAR, 0, 0, tiled=True)  40.9 us
    all_to_all x1, waiting for transfers between devices, body(): parts = lax.all_to_all(summed, PLANE, 0, 0, tiled=True)  13.1 us
    all_to_all x1, waiting for transfers between devices, body(): mine = lax.all_to_all(spread, PLANE, 0, 0, tiled=True)  13 us
    all_to_all x1, waiting for transfers between devices, body(): lax.all_to_all(back.reshape(DP * 4, BACK, 128), FAR, 0, 0, tiled=True)  11.4 us
    all_to_all x1, starting transfers between devices, body(): lax.all_to_all(back.reshape(DP * 4, BACK, 128), FAR, 0, 0, tiled=True)  5.52 us
    ppermute x1, starting transfers between devices, body(): lax.ppermute(w_away, 'core', swap)  4.86 us
    pallas_call x1, Pallas kernels, body(): pl.pallas_call(weight_kernel, out_shape=(shape((112, 4096), BF),) * 2 + (...  4.37 us
    all_to_all x1, starting transfers between devices, body(): mine = lax.all_to_all(spread, PLANE, 0, 0, tiled=True)  4.27 us
  transfers between devices with their start and end apart: 6, of which 5 were waited for; matrix products, arithmetic and copies ran while one was open for 0% of the time, Pallas kernels for 6%

profile of v5, /device:TPU:1, one launch (start us, length us, event | category | flops | bytes accessed | tf_op | source)
XLA Modules:
  0.0 126.1 jit_solution(12418928429373908364)
XLA Ops:
  0.6 1.0 select_rows.1
  1.7 40.9 %all_to_all.20 = bf16[48,24,128]{2,1,0:T(8,128)(2,1)S(1)} all-to-all(bf16[48,24,128]{2,1,0:T(8,128)(2,1)S(1)} %bitcast.9), channel_id=1, replica_groups=mesh['dp'=12,'yh'=4,'yl'=2,'x'=4,'core'=2] {'dp','yh'}, dimensions={0} | all-to-all | bytes 589824 | tf_op jit(solution)/shard_map/all_to_all | solution.py:324
  42.6 1.8 %spread_rows.1 = (bf16[8,4,128,256]{3,2,1,0:T(8,128)(2,1)}, f32[1,256]{1,0:T(1,128)S(1)}) custom-call(bf16[12,4,24,128]{3,2,1,0:T(8,128)(2,1)S(1)} %bitcast.8), custom_call_target="tpu_custom_call" | custom-call | tf_op jit(solution)/shard_map/spread_rows/pallas_call | solution.py:325
  44.4 0.0 copy-start.2
  44.4 4.3 %all-to-all-start.1 = ((bf16[8,4,128,256]{3,2,1,0:T(8,128)(2,1)}), bf16[8,4,128,256]{3,2,1,0:T(8,128)(2,1)S(1)}, u32[]{:S(2)}, u32[]{:S(2)}) async-start(bf16[8,4,128,256]{3,2,1,0:T(8,128)(2,1)} %get-tuple-element.17), calls=%async_computation.1 | async-start | bytes 4194304 | tf_op jit(solution)/shard_map/all_to_all | solution.py:334
  48.7 0.0 copy-done.2
  48.7 0.0 copy-start.3
  48.7 1.2 copy-done.3
  49.9 0.0 copy-start.4
  49.9 1.2 copy-done.4
  51.1 1.8 %sort_columns.1 = (bf16[336,2048]{1,0:T(8,128)(2,1)S(1)}, bf16[336,2048]{1,0:T(8,128)(2,1)S(1)}) custom-call(s32[1]{0:T(128)} %bitcast.1.core_ref, bf16[112,4096]{1,0:T(8,128)(2,1)S(1)} %copy-done.2, bf16[112,4096]{1,0:T(8,128)(2,1)S(1)} %copy-done.3, bf16[112,4096]{1,0:T(8,128)(2,1)S(1)} %copy-done.4), custom_call_target="tpu_custom_call" | custom-call | bytes 8000000 | tf_op jit(solution)/shard_map/sort_columns/pallas_call | solution.py:304
  52.8 0.0 copy-start
  52.9 1.1 copy-done
  53.9 4.9 %collective-permute-start.1 = (bf16[336,2048]{1,0:T(8,128)(2,1)S(1)}, bf16[336,2048]{1,0:T(8,128)(2,1)S(1)}, u32[]{:S(2)}, u32[]{:S(2)}) collective-permute-start(bf16[336,2048]{1,0:T(8,128)(2,1)S(1)} %get-tuple-element.19), channel_id=1, source_target_pairs={{0,1},{1,0},{2,3},{3,2},{4,5},{5,4},{6,7},{7,6},{8,9},{9,8},{10,11... | collective-permute-start | bytes 4128776 | tf_op jit(solution)/shard_map/ppermute | solution.py:323
  58.8 2.7 %collective-permute-done.1.w = bf16[336,2048]{1,0:T(8,128)(2,1)S(1)} collective-permute-done((bf16[336,2048]{1,0:T(8,128)(2,1)S(1)}, bf16[336,2048]{1,0:T(8,128)(2,1)S(1)}, u32[]{:S(2)}, u32[]{:S(2)}) %collective-permute-start.1) | collective-permute-done | bytes 1376288 | tf_op jit(solution)/shard_map/ppermute | solution.py:323
  61.5 0.1 hold_columns.1.w_near
  61.6 13.0 %all-to-all-done.1.mine = bf16[8,4,128,256]{3,2,1,0:T(8,128)(2,1)S(1)} async-done(((bf16[8,4,128,256]{3,2,1,0:T(8,128)(2,1)}), bf16[8,4,128,256]{3,2,1,0:T(8,128)(2,1)S(1)}, u32[]{:S(2)}, u32[]{:S(2)}) %all-to-all-start.1) | async-done | bytes 2097184 | tf_op jit(solution)/shard_map/all_to_all | solution.py:334
  74.6 0.0 copy-start.1
  74.6 0.6 features_near.1.near
  75.2 0.8 copy-done.1
  76.0 0.5 features_own.1.part
  76.5 3.0 %collective-permute-start.2 = (f32[672,256]{1,0:T(8,128)S(1)}, f32[672,256]{1,0:T(8,128)S(1)}, u32[]{:S(2)}, u32[]{:S(2)}) collective-permute-start(f32[672,256]{1,0:T(8,128)S(1)} %features_own.1.part), channel_id=1, source_target_pairs={{0,1},{1,0},{2,3},{3,2},{4,5},{5,4},{6,7},{7,6},{8,9},{9,8},{10,11... | collective-permute-start | bytes 2064392 | tf_op jit(solution)/shard_map/ppermute | solution.py:351
  79.5 1.7 %collective-permute-done.2.got = f32[672,256]{1,0:T(8,128)S(1)} collective-permute-done((f32[672,256]{1,0:T(8,128)S(1)}, f32[672,256]{1,0:T(8,128)S(1)}, u32[]{:S(2)}, u32[]{:S(2)}) %collective-permute-start.2) | collective-permute-done | bytes 688160 | tf_op jit(solution)/shard_map/ppermute | solution.py:351
  81.3 1.7 %hidden_and_input_grads.1 = (bf16[8,272,256]{2,1,0:T(8,128)(2,1)}, bf16[224,256]{1,0:T(8,128)(2,1)}) custom-call(f32[672,256]{1,0:T(8,128)S(1)} %features_own.1.part, f32[672,256]{1,0:T(8,128)S(1)} %collective-permute-done.2.got, f32[1,256]{1,0:T(1,128)S(1)} %get-tuple-element.20.prob, bf16[336,2048]{1,0:T(8,128)(2,1)S(1)} %copy-done.1, ...), custom_call_target="tpu_custom_call" | custom-call | tf_op jit(solution)/shard_map/hidden_and_input_grads/pallas_call | solution.py:352
  83.0 3.6 %all-to-all-start.2 = ((bf16[8,272,256]{2,1,0:T(8,128)(2,1)}), bf16[8,272,256]{2,1,0:T(8,128)(2,1)S(1)}, u32[]{:S(2)}, u32[]{:S(2)}) async-start(bf16[8,272,256]{2,1,0:T(8,128)(2,1)} %get-tuple-element.25), calls=%async_computation.2 | async-start | bytes 2228224 | tf_op jit(solution)/shard_map/all_to_all | solution.py:365
  86.5 0.0 copy-start.5
  86.5 2.5 %collective-permute-start = (bf16[8,4,128,256]{3,2,1,0:T(8,128)(2,1)S(1)}, bf16[8,4,128,256]{3,2,1,0:T(8,128)(2,1)}, u32[]{:S(2)}, u32[]{:S(2)}) collective-permute-start(bf16[8,4,128,256]{3,2,1,0:T(8,128)(2,1)S(1)} %all-to-all-done.1.mine), channel_id=1, source_target_pairs={{0,1},{1,0},{2,3},{3,2},{4,5},{5,4},{6,7},{7,6},{8,9},{9,8},{10,11... | collective-permute-start | bytes 6291464 | tf_op jit(solution)/shard_map/ppermute | solution.py:375
  89.0 13.1 %all-to-all-done.2.recv = bf16[8,272,256]{2,1,0:T(8,128)(2,1)S(1)} async-done(((bf16[8,272,256]{2,1,0:T(8,128)(2,1)}), bf16[8,272,256]{2,1,0:T(8,128)(2,1)S(1)}, u32[]{:S(2)}, u32[]{:S(2)}) %all-to-all-start.2) | async-done | bytes 1114144 | tf_op jit(solution)/shard_map/all_to_all | solution.py:365
  102.1 1.2 return_rows.1
  103.4 5.5 %all-to-all-start.3 = ((bf16[48,16,128]{2,1,0:T(8,128)(2,1)}), bf16[48,16,128]{2,1,0:T(8,128)(2,1)S(1)}, u32[]{:S(2)}, u32[]{:S(2)}) async-start(bf16[48,16,128]{2,1,0:T(8,128)(2,1)} %bitcast.13), calls=%async_computation.3 | async-start | bytes 393216 | tf_op jit(solution)/shard_map/all_to_all | solution.py:391
  108.9 0.0 collective-permute-done.other
  108.9 0.0 copy-done.5
  108.9 0.0 copy-start.6
  108.9 4.4 %weight_grads.1 = (bf16[112,4096]{1,0:T(8,128)(2,1)}, bf16[112,4096]{1,0:T(8,128)(2,1)}, f32[8,128]{1,0:T(8,128)S(1)}) custom-call(s32[1]{0:T(128)} %bitcast.1.core_ref, bf16[8,4,128,256]{3,2,1,0:T(8,128)(2,1)S(1)} %all-to-all-done.1.mine, bf16[8,4,128,256]{3,2,1,0:T(8,128)(2,1)} %collective-permute-done.other, bf16[224,256]{1,0:T(8,128)(2,1)S(1)} %copy-done.5), custom_call_target="tpu_custom_call" | custom-call | flops 1000 | bytes 1000 | tf_op jit(solution)/shard_map/weight_grads/pallas_call | solution.py:376
  113.3 0.0 copy-done.6
  113.3 0.5 masks.1
  113.8 11.4 %all-to-all-done.3 = bf16[48,16,128]{2,1,0:T(8,128)(2,1)S(1)} async-done(((bf16[48,16,128]{2,1,0:T(8,128)(2,1)}), bf16[48,16,128]{2,1,0:T(8,128)(2,1)S(1)}, u32[]{:S(2)}, u32[]{:S(2)}) %all-to-all-start.3) | async-done | bytes 196640 | tf_op jit(solution)/shard_map/all_to_all | solution.py:391
  125.2 0.8 combine.1
Async XLA Ops:
  44.4 4.3 %copy-start.2 = (bf16[112,4096]{1,0:T(8,128)(2,1)S(1)}, bf16[112,4096]{1,0:T(8,128)(2,1)}, u32[]{:S(2)}) copy-start(bf16[112,4096]{1,0:T(8,128)(2,1)} %wg.1) | copy-start | bytes 2752516
  44.4 30.2 %all-to-all-start.1 = ((bf16[8,4,128,256]{3,2,1,0:T(8,128)(2,1)}), bf16[8,4,128,256]{3,2,1,0:T(8,128)(2,1)S(1)}, u32[]{:S(2)}, u32[]{:S(2)}) async-start(bf16[8,4,128,256]{3,2,1,0:T(8,128)(2,1)} %get-tuple-element.17), calls=%async_computation.1 | async-start | bytes 4194304 | tf_op jit(solution)/shard_map/all_to_all | solution.py:334
  48.7 1.2 copy-start.3
  49.9 1.2 copy-start.4
  52.8 1.1 copy-start
  53.9 7.6 %collective-permute-start.1 = (bf16[336,2048]{1,0:T(8,128)(2,1)S(1)}, bf16[336,2048]{1,0:T(8,128)(2,1)S(1)}, u32[]{:S(2)}, u32[]{:S(2)}) collective-permute-start(bf16[336,2048]{1,0:T(8,128)(2,1)S(1)} %get-tuple-element.19), channel_id=1, source_target_pairs={{0,1},{1,0},{2,3},{3,2},{4,5},{5,4},{6,7},{7,6},{8,9},{9,8},{10,11... | collective-permute-start | bytes 4128776 | tf_op jit(solution)/shard_map/ppermute | solution.py:323
  74.6 1.3 %copy-start.1 = (bf16[336,2048]{1,0:T(8,128)(2,1)S(1)}, bf16[336,2048]{1,0:T(8,128)(2,1)}, u32[]{:S(2)}) copy-start(bf16[336,2048]{1,0:T(8,128)(2,1)} %copy-done) | copy-start | bytes 4128772
  76.5 4.7 %collective-permute-start.2 = (f32[672,256]{1,0:T(8,128)S(1)}, f32[672,256]{1,0:T(8,128)S(1)}, u32[]{:S(2)}, u32[]{:S(2)}) collective-permute-start(f32[672,256]{1,0:T(8,128)S(1)} %features_own.1.part), channel_id=1, source_target_pairs={{0,1},{1,0},{2,3},{3,2},{4,5},{5,4},{6,7},{7,6},{8,9},{9,8},{10,11... | collective-permute-start | bytes 2064392 | tf_op jit(solution)/shard_map/ppermute | solution.py:351
  83.0 19.2 %all-to-all-start.2 = ((bf16[8,272,256]{2,1,0:T(8,128)(2,1)}), bf16[8,272,256]{2,1,0:T(8,128)(2,1)S(1)}, u32[]{:S(2)}, u32[]{:S(2)}) async-start(bf16[8,272,256]{2,1,0:T(8,128)(2,1)} %get-tuple-element.25), calls=%async_computation.2 | async-start | bytes 2228224 | tf_op jit(solution)/shard_map/all_to_all | solution.py:365
  86.5 22.4 %copy-start.5 = (bf16[224,256]{1,0:T(8,128)(2,1)S(1)}, bf16[224,256]{1,0:T(8,128)(2,1)}, u32[]{:S(2)}) copy-start(bf16[224,256]{1,0:T(8,128)(2,1)} %get-tuple-element.21.pre) | copy-start | bytes 344068
  86.5 22.4 %collective-permute-start = (bf16[8,4,128,256]{3,2,1,0:T(8,128)(2,1)S(1)}, bf16[8,4,128,256]{3,2,1,0:T(8,128)(2,1)}, u32[]{:S(2)}, u32[]{:S(2)}) collective-permute-start(bf16[8,4,128,256]{3,2,1,0:T(8,128)(2,1)S(1)} %all-to-all-done.1.mine), channel_id=1, source_target_pairs={{0,1},{1,0},{2,3},{3,2},{4,5},{5,4},{6,7},{7,6},{8,9},{9,8},{10,11... | collective-permute-start | bytes 6291464 | tf_op jit(solution)/shard_map/ppermute | solution.py:375
  103.4 21.8 %all-to-all-start.3 = ((bf16[48,16,128]{2,1,0:T(8,128)(2,1)}), bf16[48,16,128]{2,1,0:T(8,128)(2,1)S(1)}, u32[]{:S(2)}, u32[]{:S(2)}) async-start(bf16[48,16,128]{2,1,0:T(8,128)(2,1)} %bitcast.13), calls=%async_computation.3 | async-start | bytes 393216 | tf_op jit(solution)/shard_map/all_to_all | solution.py:391
  108.9 4.4 %copy-start.6 = (s32[32,2]{0,1:T(2,128)S(1)}, s32[32,2]{0,1:T(2,128)}, u32[]{:S(2)}) copy-start(s32[32,2]{0,1:T(2,128)} %param.9) | copy-start | bytes 772
